TPU v7x, 256 devices: a whole 4x4x8 slice. The times are simulated.
256 devices in a mesh: grp: 8 (over y, x_lo), ep: 32 (over x_hi, z, core).
Axes of the slice: x: 4 (x_hi: 2, x_lo: 2; x = x_hi * 2 + x_lo), y: 4, z: 8, core: 2. Of those that a mesh axis runs over, the one named last changes fastest.
Arguments:
- queries: bfloat16 [8, 32, 384, 5120], P('grp', 'ep'), may hold values from -8 to 8
- suffix_kv: bfloat16 [8, 32, 2, 384, 1024], P('grp', 'ep'), may hold values from -6 to 6
- slot_page_cache: bfloat16 [8, 32, 16, 2, 16, 1024], P('grp', 'ep'), may hold values from -6 to 6
- holder: int32 [8, 32], replicated, may hold values from 0 to 7, as said below
- page_slots: int32 [8, 32, 32], replicated, may hold values from 0 to 15
- page_count: int32 [8, 32], replicated, may hold values from 1 to 32
Outputs:
- attended: bfloat16 [8, 32, 384, 5120], P('grp', 'ep')
Inputs may be any that keep to these rules, and one draw needn't show every extreme that they name: In every group exactly 8 requests share one holder group and no holder group serves more than 8 requests of one group.
All inputs are finite; a program needn't handle non-finite values.
Results may differ from a plain program's by a relative error of at most 0.005.
Values may be sent and summed in bfloat16 or wider, within the bound.
No kernel may reach another device: no remote copies, remote signals or barrier semaphores. Data moves between devices by JAX's collectives and lax.ppermute only.
A program may use at most 128 MiB of HBM per device.

v0:
```python
import jax
import jax.numpy as jnp
from jax import lax
from jax.sharding import PartitionSpec as P

QUERY_HEAD_COUNT = 40
KEY_VALUE_HEADS = 8
HEAD_SIZE = 128


def attend(rows_of_queries, pulled, suffix_pair, page_total):
    suffix_length = rows_of_queries.shape[0]
    page_number, pair_dim, page_len, kv_width = pulled.shape
    prefix_len = page_number * page_len
    prefix_kv = jnp.transpose(pulled, (1, 0, 2, 3)).reshape(2, prefix_len, kv_width)
    key_value_pair = jnp.concatenate([prefix_kv, suffix_pair], axis=1)
    total_keys = prefix_len + suffix_length
    group_width = QUERY_HEAD_COUNT // KEY_VALUE_HEADS
    heads_of_queries = rows_of_queries.reshape(
        suffix_length, KEY_VALUE_HEADS, group_width, HEAD_SIZE
    ).transpose(1, 2, 0, 3)
    heads_of_keys = (
        key_value_pair[0].reshape(total_keys, KEY_VALUE_HEADS, HEAD_SIZE).transpose(1, 0, 2)
    )
    heads_of_values = (
        key_value_pair[1].reshape(total_keys, KEY_VALUE_HEADS, HEAD_SIZE).transpose(1, 0, 2)
    )
    key_pos = jnp.arange(total_keys)
    query_pos = jnp.arange(suffix_length)
    in_prefix = key_pos[None, :] // page_len < page_total
    in_suffix = key_pos[None, :] - prefix_len <= query_pos[:, None]
    allowed = jnp.where(key_pos[None, :] < prefix_len, in_prefix, in_suffix)
    scale = 1.0 / HEAD_SIZE**0.5

    def one_head(operands):
        q_head, k_head, v_head = operands
        scores = (
            jnp.einsum("gsd,td->gst", q_head, k_head, preferred_element_type=jnp.float32) * scale
        )
        scores = jnp.where(allowed[None], scores, -1e30)
        top_score = jnp.max(scores, axis=-1, keepdims=True)
        raised = jnp.where(allowed[None], jnp.exp(scores - top_score), 0.0)
        total = jnp.sum(raised, axis=-1, keepdims=True)
        weights = (raised / total).astype(jnp.bfloat16)
        return jnp.einsum("gst,td->gsd", weights, v_head, preferred_element_type=jnp.float32)

    mixed = lax.map(one_head, (heads_of_queries, heads_of_keys, heads_of_values))
    mixed = mixed.transpose(2, 0, 1, 3).reshape(suffix_length, QUERY_HEAD_COUNT * HEAD_SIZE)
    return mixed.astype(jnp.bfloat16)


def local(queries, suffix_kv, slot_page_cache, holder, page_slots, page_count):
    group_now = lax.axis_index("grp")
    lane_now = lax.axis_index("ep")
    lane_total = holder.shape[1]
    lane_ids = jnp.arange(lane_total)
    page_rows = slot_page_cache[0, 0]
    my_slots = page_slots[:, :, lane_now]
    owned_here = holder == group_now
    mine_h = holder[group_now]
    gathered = page_rows[my_slots]
    outgoing = jnp.where(owned_here[:, :, None, None, None], gathered, jnp.zeros_like(gathered))
    arrived = lax.all_to_all(outgoing, "grp", split_axis=0, concat_axis=0, tiled=True)
    forward = arrived[mine_h, lane_ids]
    pulled = lax.all_to_all(forward, "ep", split_axis=0, concat_axis=0, tiled=True)
    page_total = page_count[group_now, lane_now]
    result = attend(queries[0, 0], pulled, suffix_kv[0, 0], page_total)
    return result[None, None]


def solution(mesh):
    return jax.shard_map(
        local,
        mesh=mesh,
        in_specs=(
            P("grp", "ep", None, None),
            P("grp", "ep", None, None, None),
            P("grp", "ep", None, None, None, None),
            P(),
            P(),
            P(),
        ),
        out_specs=P("grp", "ep", None, None),
        check_vma=False,
    )
```

profile of v0, /device:TPU:32, one launch (start us, length us, event | category | flops | bytes accessed | tf_op | source)
XLA Modules:
  0.0 401.8 jit_solution(2560535638944711100)
XLA Ops:
  0.0 0.0 copy-start
  0.0 1.3 fusion.42
  1.3 0.1 reshape.99
  1.4 0.0 copy-done
  1.4 0.0 copy-start.3
  1.4 9.7 %gather_fusion = bf16[256,2,16,1024]{3,2,1,0:T(8,128)(2,1)} fusion(bf16[16,2,16,1024]{3,2,1,0:T(8,128)(2,1)S(1)} %bitcast.69, s32[1024]{0:T(1024)S(1)} %pad_clamp_fusion), kind=kCustom, calls=%fused_computation | custom fusion | bytes 33555456 | tf_op jit(solution)/shard_map/gather | solution.py:61
  11.1 0.0 copy-done.3
  11.1 14.0 %broadcast_select_fusion = bf16[8,32,2,16,1024]{4,3,2,1,0:T(8,128)(2,1)} fusion(bf16[8,32,2,16,1024]{4,3,2,1,0:T(8,128)(2,1)} %bitcast.70, pred[8,32]{1,0:T(8,128)(4,1)S(1)} %broadcast_compare_fusion), kind=kLoop, calls=%fused_computation.33 | loop fusion | flops 8388608 | bytes 33554688 | tf_op jit(solution)/shard_map/jit(_where)/select_n | solution.py:62
  25.1 5.7 %all-to-all-start = ((bf16[8,32,2,16,1024]{4,3,2,1,0:T(8,128)(2,1)}), bf16[8,32,2,16,1024]{4,3,2,1,0:T(8,128)(2,1)}, u32[]{:S(2)}, u32[]{:S(2)}) async-start(bf16[8,32,2,16,1024]{4,3,2,1,0:T(8,128)(2,1)} %broadcast_select_fusion), calls=%async_computation | async-start | bytes 33554432 | tf_op jit(solution)/shard_map/all_to_all | solution.py:63
  30.9 184.6 %all-to-all-done = bf16[8,32,2,16,1024]{4,3,2,1,0:T(8,128)(2,1)} async-done(((bf16[8,32,2,16,1024]{4,3,2,1,0:T(8,128)(2,1)}), bf16[8,32,2,16,1024]{4,3,2,1,0:T(8,128)(2,1)}, u32[]{:S(2)}, u32[]{:S(2)}) %all-to-all-start) | async-done | bytes 16777248 | tf_op jit(solution)/shard_map/all_to_all | solution.py:63
  215.5 7.8 %gather_fusion.1 = bf16[32,2,16,1024]{3,2,1,0:T(8,128)(2,1)} fusion(bf16[8,32,2,16,1024]{4,3,2,1,0:T(8,128)(2,1)} %all-to-all-done, s32[32]{0:T(128)S(1)} %fusion.50), kind=kCustom, calls=%fused_computation.1 | custom fusion | bytes 4194560 | tf_op jit(solution)/shard_map/gather | solution.py:64
  223.3 11.1 %all-to-all-start.1 = ((bf16[32,2,16,1024]{3,2,1,0:T(8,128)(2,1)}), bf16[32,2,16,1024]{3,2,1,0:T(8,128)(2,1)S(1)}, u32[]{:S(2)}, u32[]{:S(2)}) async-start(bf16[32,2,16,1024]{3,2,1,0:T(8,128)(2,1)} %gather_fusion.1), calls=%async_computation.1 | async-start | bytes 4194304 | tf_op jit(solution)/shard_map/all_to_all | solution.py:65
  234.4 1.3 dynamic_slice.20
  235.7 6.3 %copy.16 = bf16[1,1,384,5120]{2,3,1,0:T(8,128)(2,1)} copy(bf16[1,1,384,5120]{3,2,1,0:T(8,128)(2,1)} %param.8) | data formatting | bytes 7864320 | tf_op args[0]
  242.0 0.6 fusion.43
  242.6 44.8 %all-to-all-done.1 = bf16[32,2,16,1024]{3,2,1,0:T(8,128)(2,1)S(1)} async-done(((bf16[32,2,16,1024]{3,2,1,0:T(8,128)(2,1)}), bf16[32,2,16,1024]{3,2,1,0:T(8,128)(2,1)S(1)}, u32[]{:S(2)}, u32[]{:S(2)}) %all-to-all-start.1) | async-done | bytes 2097184 | tf_op jit(solution)/shard_map/all_to_all | solution.py:65
  287.4 0.2 copy.17
  287.6 1.2 copy-done.2
  288.8 1.5 pad_maximum_fusion
  290.3 3.8 copy.18
  294.1 2.5 copy.19
  296.6 98.8 %while.11 = (s32[]{:T(128)}, bf16[8,5,384,128]{2,3,1,0:T(8,128)(2,1)}, bf16[8,5,384,128]{2,3,1,0:T(8,128)(2,1)}, bf16[8,896,128]{1,2,0:T(8,128)(2,1)}, bf16[8,89...) while((s32[]{:T(128)}, ...), condition=%wide.region_3.4_spmd.clone, body=%wide.region_0.3_spmd.clone.sunk | while | flops 893535104 | bytes 16750941 | solution.py:47
  296.6 0.2 fusion.69
  296.8 7.1 %fusion.70 = (f32[5,384]{1,0:T(8,128)S(1)}, f32[5,384,896]{2,1,0:T(8,128)}) fusion(pred[384,896]{1,0:T(8,128)(4,1)S(1)} %fusion.69, bf16[8,5,384,128]{2,3,1,0:T(8,128)(2,1)} %get-tuple-element.170, s32[]{:T(128)} %get-tuple-element.159, bf16[8,896,128]{1,2,0:T(8,128)(2,1)} %get-tuple-element.171), kind=kOutput, calls=%fused_computation.57.clone.1 | convolution fusion | flops 449004416 | bytes 8299008 | tf_op jit(solution)/shard_map/while/body/eval_jaxpr/sub | solution.py:42
  304.0 5.0 %fusion.71 = bf16[8,5,384,128]{2,3,1,0:T(8,128)(2,1)} fusion(bf16[8,5,384,128]{2,3,1,0:T(8,128)(2,1)} %get-tuple-element.160, s32[]{:T(128)} %get-tuple-element.159, f32[5,384,896]{2,1,0:T(8,128)} %get-tuple-element.148, f32[5,384]{1,0:T(8,128)S(1)} %get-tuple-element.149, bf16[8,896,128]{1,2,0:T(8,128)(2,1)} %get-tuple-element.172), kind=kOutput, calls=%fused_computation.15.clone.1 | convolution fusion | flops 443842560 | bytes 8102400 | tf_op jit(solution)/shard_map/while/body/eval_jaxpr/gst,td->gsd/dot_general | solution.py:45
  308.9 0.2 fusion.69
  309.2 7.1 %fusion.70 = (f32[5,384]{1,0:T(8,128)S(1)}, f32[5,384,896]{2,1,0:T(8,128)}) fusion(pred[384,896]{1,0:T(8,128)(4,1)S(1)} %fusion.69, bf16[8,5,384,128]{2,3,1,0:T(8,128)(2,1)} %get-tuple-element.170, s32[]{:T(128)} %get-tuple-element.159, bf16[8,896,128]{1,2,0:T(8,128)(2,1)} %get-tuple-element.171), kind=kOutput, calls=%fused_computation.57.clone.1 | convolution fusion | flops 449004416 | bytes 8299008 | tf_op jit(solution)/shard_map/while/body/eval_jaxpr/sub | solution.py:42
  316.3 4.9 %fusion.71 = bf16[8,5,384,128]{2,3,1,0:T(8,128)(2,1)} fusion(bf16[8,5,384,128]{2,3,1,0:T(8,128)(2,1)} %get-tuple-element.160, s32[]{:T(128)} %get-tuple-element.159, f32[5,384,896]{2,1,0:T(8,128)} %get-tuple-element.148, f32[5,384]{1,0:T(8,128)S(1)} %get-tuple-element.149, bf16[8,896,128]{1,2,0:T(8,128)(2,1)} %get-tuple-element.172), kind=kOutput, calls=%fused_computation.15.clone.1 | convolution fusion | flops 443842560 | bytes 8102400 | tf_op jit(solution)/shard_map/while/body/eval_jaxpr/gst,td->gsd/dot_general | solution.py:45
  321.3 0.2 fusion.69
  321.5 7.1 %fusion.70 = (f32[5,384]{1,0:T(8,128)S(1)}, f32[5,384,896]{2,1,0:T(8,128)}) fusion(pred[384,896]{1,0:T(8,128)(4,1)S(1)} %fusion.69, bf16[8,5,384,128]{2,3,1,0:T(8,128)(2,1)} %get-tuple-element.170, s32[]{:T(128)} %get-tuple-element.159, bf16[8,896,128]{1,2,0:T(8,128)(2,1)} %get-tuple-element.171), kind=kOutput, calls=%fused_computation.57.clone.1 | convolution fusion | flops 449004416 | bytes 8299008 | tf_op jit(solution)/shard_map/while/body/eval_jaxpr/sub | solution.py:42
  328.7 5.0 %fusion.71 = bf16[8,5,384,128]{2,3,1,0:T(8,128)(2,1)} fusion(bf16[8,5,384,128]{2,3,1,0:T(8,128)(2,1)} %get-tuple-element.160, s32[]{:T(128)} %get-tuple-element.159, f32[5,384,896]{2,1,0:T(8,128)} %get-tuple-element.148, f32[5,384]{1,0:T(8,128)S(1)} %get-tuple-element.149, bf16[8,896,128]{1,2,0:T(8,128)(2,1)} %get-tuple-element.172), kind=kOutput, calls=%fused_computation.15.clone.1 | convolution fusion | flops 443842560 | bytes 8102400 | tf_op jit(solution)/shard_map/while/body/eval_jaxpr/gst,td->gsd/dot_general | solution.py:45
  333.6 0.2 fusion.69
  333.9 7.1 %fusion.70 = (f32[5,384]{1,0:T(8,128)S(1)}, f32[5,384,896]{2,1,0:T(8,128)}) fusion(pred[384,896]{1,0:T(8,128)(4,1)S(1)} %fusion.69, bf16[8,5,384,128]{2,3,1,0:T(8,128)(2,1)} %get-tuple-element.170, s32[]{:T(128)} %get-tuple-element.159, bf16[8,896,128]{1,2,0:T(8,128)(2,1)} %get-tuple-element.171), kind=kOutput, calls=%fused_computation.57.clone.1 | convolution fusion | flops 449004416 | bytes 8299008 | tf_op jit(solution)/shard_map/while/body/eval_jaxpr/sub | solution.py:42
  341.0 5.0 %fusion.71 = bf16[8,5,384,128]{2,3,1,0:T(8,128)(2,1)} fusion(bf16[8,5,384,128]{2,3,1,0:T(8,128)(2,1)} %get-tuple-element.160, s32[]{:T(128)} %get-tuple-element.159, f32[5,384,896]{2,1,0:T(8,128)} %get-tuple-element.148, f32[5,384]{1,0:T(8,128)S(1)} %get-tuple-element.149, bf16[8,896,128]{1,2,0:T(8,128)(2,1)} %get-tuple-element.172), kind=kOutput, calls=%fused_computation.15.clone.1 | convolution fusion | flops 443842560 | bytes 8102400 | tf_op jit(solution)/shard_map/while/body/eval_jaxpr/gst,td->gsd/dot_general | solution.py:45
  346.0 0.2 fusion.69
  346.3 7.1 %fusion.70 = (f32[5,384]{1,0:T(8,128)S(1)}, f32[5,384,896]{2,1,0:T(8,128)}) fusion(pred[384,896]{1,0:T(8,128)(4,1)S(1)} %fusion.69, bf16[8,5,384,128]{2,3,1,0:T(8,128)(2,1)} %get-tuple-element.170, s32[]{:T(128)} %get-tuple-element.159, bf16[8,896,128]{1,2,0:T(8,128)(2,1)} %get-tuple-element.171), kind=kOutput, calls=%fused_computation.57.clone.1 | convolution fusion | flops 449004416 | bytes 8299008 | tf_op jit(solution)/shard_map/while/body/eval_jaxpr/sub | solution.py:42
  353.4 5.0 %fusion.71 = bf16[8,5,384,128]{2,3,1,0:T(8,128)(2,1)} fusion(bf16[8,5,384,128]{2,3,1,0:T(8,128)(2,1)} %get-tuple-element.160, s32[]{:T(128)} %get-tuple-element.159, f32[5,384,896]{2,1,0:T(8,128)} %get-tuple-element.148, f32[5,384]{1,0:T(8,128)S(1)} %get-tuple-element.149, bf16[8,896,128]{1,2,0:T(8,128)(2,1)} %get-tuple-element.172), kind=kOutput, calls=%fused_computation.15.clone.1 | convolution fusion | flops 443842560 | bytes 8102400 | tf_op jit(solution)/shard_map/while/body/eval_jaxpr/gst,td->gsd/dot_general | solution.py:45
  358.4 0.2 fusion.69
  358.7 7.1 %fusion.70 = (f32[5,384]{1,0:T(8,128)S(1)}, f32[5,384,896]{2,1,0:T(8,128)}) fusion(pred[384,896]{1,0:T(8,128)(4,1)S(1)} %fusion.69, bf16[8,5,384,128]{2,3,1,0:T(8,128)(2,1)} %get-tuple-element.170, s32[]{:T(128)} %get-tuple-element.159, bf16[8,896,128]{1,2,0:T(8,128)(2,1)} %get-tuple-element.171), kind=kOutput, calls=%fused_computation.57.clone.1 | convolution fusion | flops 449004416 | bytes 8299008 | tf_op jit(solution)/shard_map/while/body/eval_jaxpr/sub | solution.py:42
  365.8 5.0 %fusion.71 = bf16[8,5,384,128]{2,3,1,0:T(8,128)(2,1)} fusion(bf16[8,5,384,128]{2,3,1,0:T(8,128)(2,1)} %get-tuple-element.160, s32[]{:T(128)} %get-tuple-element.159, f32[5,384,896]{2,1,0:T(8,128)} %get-tuple-element.148, f32[5,384]{1,0:T(8,128)S(1)} %get-tuple-element.149, bf16[8,896,128]{1,2,0:T(8,128)(2,1)} %get-tuple-element.172), kind=kOutput, calls=%fused_computation.15.clone.1 | convolution fusion | flops 443842560 | bytes 8102400 | tf_op jit(solution)/shard_map/while/body/eval_jaxpr/gst,td->gsd/dot_general | solution.py:45
  370.8 0.2 fusion.69
  371.0 7.1 %fusion.70 = (f32[5,384]{1,0:T(8,128)S(1)}, f32[5,384,896]{2,1,0:T(8,128)}) fusion(pred[384,896]{1,0:T(8,128)(4,1)S(1)} %fusion.69, bf16[8,5,384,128]{2,3,1,0:T(8,128)(2,1)} %get-tuple-element.170, s32[]{:T(128)} %get-tuple-element.159, bf16[8,896,128]{1,2,0:T(8,128)(2,1)} %get-tuple-element.171), kind=kOutput, calls=%fused_computation.57.clone.1 | convolution fusion | flops 449004416 | bytes 8299008 | tf_op jit(solution)/shard_map/while/body/eval_jaxpr/sub | solution.py:42
  378.1 4.9 %fusion.71 = bf16[8,5,384,128]{2,3,1,0:T(8,128)(2,1)} fusion(bf16[8,5,384,128]{2,3,1,0:T(8,128)(2,1)} %get-tuple-element.160, s32[]{:T(128)} %get-tuple-element.159, f32[5,384,896]{2,1,0:T(8,128)} %get-tuple-element.148, f32[5,384]{1,0:T(8,128)S(1)} %get-tuple-element.149, bf16[8,896,128]{1,2,0:T(8,128)(2,1)} %get-tuple-element.172), kind=kOutput, calls=%fused_computation.15.clone.1 | convolution fusion | flops 443842560 | bytes 8102400 | tf_op jit(solution)/shard_map/while/body/eval_jaxpr/gst,td->gsd/dot_general | solution.py:45
  383.1 0.2 fusion.69
  383.3 7.1 %fusion.70 = (f32[5,384]{1,0:T(8,128)S(1)}, f32[5,384,896]{2,1,0:T(8,128)}) fusion(pred[384,896]{1,0:T(8,128)(4,1)S(1)} %fusion.69, bf16[8,5,384,128]{2,3,1,0:T(8,128)(2,1)} %get-tuple-element.170, s32[]{:T(128)} %get-tuple-element.159, bf16[8,896,128]{1,2,0:T(8,128)(2,1)} %get-tuple-element.171), kind=kOutput, calls=%fused_computation.57.clone.1 | convolution fusion | flops 449004416 | bytes 8299008 | tf_op jit(solution)/shard_map/while/body/eval_jaxpr/sub | solution.py:42
  390.5 5.0 %fusion.71 = bf16[8,5,384,128]{2,3,1,0:T(8,128)(2,1)} fusion(bf16[8,5,384,128]{2,3,1,0:T(8,128)(2,1)} %get-tuple-element.160, s32[]{:T(128)} %get-tuple-element.159, f32[5,384,896]{2,1,0:T(8,128)} %get-tuple-element.148, f32[5,384]{1,0:T(8,128)S(1)} %get-tuple-element.149, bf16[8,896,128]{1,2,0:T(8,128)(2,1)} %get-tuple-element.172), kind=kOutput, calls=%fused_computation.15.clone.1 | convolution fusion | flops 443842560 | bytes 8102400 | tf_op jit(solution)/shard_map/while/body/eval_jaxpr/gst,td->gsd/dot_general | solution.py:45
  395.5 6.4 %copy.24 = bf16[1,1,384,5120]{3,2,1,0:T(8,128)(2,1)} copy(bf16[1,1,384,5120]{2,3,1,0:T(8,128)(2,1)} %bitcast.74) | data formatting | bytes 7864320 | tf_op jit(solution)/shard_map/convert_element_type | solution.py:49
  401.8 0.0 copy-done.1
  (7 shorter events, 0.0 us)
Async XLA Ops:
  0.0 1.4 copy-start
  1.4 9.7 %copy-start.3 = (s32[8,32]{1,0:T(8,128)S(1)}, s32[8,32]{1,0:T(8,128)}, u32[]{:S(2)}) copy-start(s32[8,32]{1,0:T(8,128)} %param.11) | copy-start | bytes 3076
  25.1 190.4 %all-to-all-start = ((bf16[8,32,2,16,1024]{4,3,2,1,0:T(8,128)(2,1)}), bf16[8,32,2,16,1024]{4,3,2,1,0:T(8,128)(2,1)}, u32[]{:S(2)}, u32[]{:S(2)}) async-start(bf16[8,32,2,16,1024]{4,3,2,1,0:T(8,128)(2,1)} %broadcast_select_fusion), calls=%async_computation | async-start | bytes 33554432 | tf_op jit(solution)/shard_map/all_to_all | solution.py:63
  223.3 64.1 %all-to-all-start.1 = ((bf16[32,2,16,1024]{3,2,1,0:T(8,128)(2,1)}), bf16[32,2,16,1024]{3,2,1,0:T(8,128)(2,1)S(1)}, u32[]{:S(2)}, u32[]{:S(2)}) async-start(bf16[32,2,16,1024]{3,2,1,0:T(8,128)(2,1)} %gather_fusion.1), calls=%async_computation.1 | async-start | bytes 4194304 | tf_op jit(solution)/shard_map/all_to_all | solution.py:65
  287.4 1.4 copy-start.2
  395.5 6.4 %copy-start.1 = (bf16[1,1,16,2,16,1024]{5,4,3,2,1,0:T(8,128)(2,1)S(1)}, bf16[1,1,16,2,16,1024]{5,4,3,2,1,0:T(8,128)(2,1)}, u32[]{:S(2)}) copy-start(bf16[1,1,16,2,16,1024]{5,4,3,2,1,0:T(8,128)(2,1)} %param.10) | copy-start | bytes 3145732
where the time goes:
time: 403 us; the launch traced here: 402 us
  waiting for transfers between devices  229 us (57%)
  matrix products  96.9 us (24%)
  local copies, waits for them, and re-layouts  39.2 us (10%)
  other arithmetic  19.3 us (5%)
  starting transfers between devices  16.9 us (4%)
    all_to_all x1, waiting for transfers between devices, local(): lax.all_to_all(outgoing, 'grp', split_axis=0, concat_axis=0, tiled=True)  185 us
    sub x8, matrix products, one_head(): raised = jnp.where(allowed[None], jnp.exp(scores - top_score), 0.0)  57.2 us
    all_to_all x1, waiting for transfers between devices, local(): lax.all_to_all(forward, 'ep', split_axis=0, concat_axis=0, tiled=True)  44.8 us
    dot_general x8, matrix products, one_head(): jnp.einsum('gst,td->gsd', weights, v_head, preferred_element_type=jnp.flo...  39.7 us
    select_n x1, other arithmetic, local(): jnp.where(owned_here[:, :, None, None, None], gathered, jnp.zeros_like(ga...  14 us
    all_to_all x1, starting transfers between devices, local(): lax.all_to_all(forward, 'ep', split_axis=0, concat_axis=0, tiled=True)  11.1 us
    gather x1, local copies, waits for them, and re-layouts, local(): gathered = page_rows[my_slots]  9.72 us
  transfers between devices with their start and end apart: 2, of which 2 were waited for; matrix products, arithmetic and copies ran while one was open for 2% of the time, Pallas kernels for 0%

commit v1 on v0

v1 whole, which is shorter than its diff:
```python
import functools
import math

import jax
import jax.numpy as jnp
from jax import lax
from jax.experimental import pallas as pl
from jax.experimental.pallas import tpu as pltpu
from jax.sharding import PartitionSpec as P

HEAD = 128
KV_HEADS = 8
GROUP_HEADS = 5
PAGE = 16
CAP = 8
TILE = 128
SMEM = pltpu.MemorySpace.SMEM
NEG = -1e30


def pack_kernel(n_grp, n_ep, holder_ref, slots_ref, cache_ref, out_ref, count_ref, sem):
    me = lax.axis_index("grp")
    lane = lax.axis_index("ep")

    def group(g, carry):
        count_ref[g] = 0

        def request(e, carry):
            @pl.when(holder_ref[g, e] == me)
            def _():
                k = count_ref[g]
                at = g * CAP + k
                pltpu.make_async_copy(cache_ref.at[slots_ref[g, e]], out_ref.at[at], sem.at[at]).start()
                count_ref[g] = k + 1

            return carry

        return lax.fori_loop(0, n_ep, request, carry, unroll=8)

    lax.fori_loop(0, n_grp, group, 0)

    def drain(at, carry):
        @pl.when(lax.rem(at, CAP) < count_ref[at // CAP])
        def _():
            pltpu.make_async_copy(cache_ref.at[0], out_ref.at[at], sem.at[at]).wait()

        return carry

    lax.fori_loop(0, n_grp * CAP, drain, 0)


def pack(holder, slots, cache):
    n_grp, n_ep = holder.shape
    return pl.pallas_call(
        functools.partial(pack_kernel, n_grp, n_ep),
        out_shape=jax.ShapeDtypeStruct((n_grp * CAP,) + cache.shape[1:], cache.dtype),
        in_specs=[
            pl.BlockSpec(memory_space=SMEM),
            pl.BlockSpec(memory_space=SMEM),
            pl.BlockSpec(memory_space=pl.ANY),
        ],
        out_specs=pl.BlockSpec(memory_space=pl.ANY),
        scratch_shapes=[pltpu.SMEM((n_grp,), jnp.int32), pltpu.SemaphoreType.DMA((n_grp * CAP,))],
        name="pack_pages",
    )(holder, slots, cache)


def select_kernel(n_grp, n_ep, holder_ref, arrived_ref, out_ref, count_ref, sem):
    me = lax.axis_index("grp")

    def clear(h, carry):
        count_ref[h] = 0
        return carry

    lax.fori_loop(0, n_grp, clear, 0, unroll=True)

    def request(e, carry):
        h = holder_ref[me, e]
        k = count_ref[h]
        pltpu.make_async_copy(arrived_ref.at[h * CAP + k], out_ref.at[e], sem.at[e]).start()
        count_ref[h] = k + 1
        return carry

    lax.fori_loop(0, n_ep, request, 0, unroll=4)

    def drain(e, carry):
        pltpu.make_async_copy(arrived_ref.at[0], out_ref.at[e], sem.at[e]).wait()
        return carry

    lax.fori_loop(0, n_ep, drain, 0)


def select(holder, arrived):
    n_grp, n_ep = holder.shape
    return pl.pallas_call(
        functools.partial(select_kernel, n_grp, n_ep),
        out_shape=jax.ShapeDtypeStruct((n_ep,) + arrived.shape[1:], arrived.dtype),
        in_specs=[pl.BlockSpec(memory_space=SMEM), pl.BlockSpec(memory_space=pl.ANY)],
        out_specs=pl.BlockSpec(memory_space=pl.ANY),
        scratch_shapes=[pltpu.SMEM((n_grp,), jnp.int32), pltpu.SemaphoreType.DMA((n_ep,))],
        name="select_pages",
    )(holder, arrived)


def attend_kernel(pages, q_ref, pulled_ref, suffix_ref, count_ref, o_ref):
    prefix = pages * PAGE
    tokens = q_ref.shape[0]
    valid = count_ref[lax.axis_index("grp"), lax.axis_index("ep")] * PAGE
    ok = lax.broadcasted_iota(jnp.int32, (prefix, HEAD), 0) < valid
    k_pre = pulled_ref[:, 0].reshape(prefix, HEAD).astype(jnp.float32)
    k_pre = jnp.where(ok, k_pre, k_pre[0:1, :]).astype(jnp.bfloat16)
    v_pre = pulled_ref[:, 1].reshape(prefix, HEAD).astype(jnp.float32)
    v_pre = jnp.where(ok, v_pre, 0.0).astype(jnp.bfloat16)
    one_pre = jnp.where(ok, 1.0, 0.0).astype(jnp.bfloat16)
    keys = jnp.concatenate([k_pre, suffix_ref[0]], axis=0)
    values = jnp.concatenate(
        [
            jnp.concatenate([v_pre, one_pre], axis=1),
            jnp.concatenate([suffix_ref[1], jnp.ones((tokens, HEAD), jnp.bfloat16)], axis=1),
        ],
        axis=0,
    )
    scale = math.log2(math.e) / math.sqrt(HEAD)
    rows = GROUP_HEADS * TILE
    tri = lax.rem(lax.broadcasted_iota(jnp.int32, (rows, TILE), 0), TILE) >= lax.broadcasted_iota(
        jnp.int32, (rows, TILE), 1
    )

    for i in range(tokens // TILE):
        span = slice(i * TILE, (i + 1) * TILE)
        total = prefix + (i + 1) * TILE
        q = jnp.concatenate([q_ref[span, n * HEAD : (n + 1) * HEAD] for n in range(GROUP_HEADS)], axis=0)
        s = lax.dot_general(q, keys[:total], (((1,), (1,)), ((), ())), preferred_element_type=jnp.float32)
        s = jnp.concatenate([s[:, : total - TILE], jnp.where(tri, s[:, total - TILE :], NEG)], axis=1)
        top = jnp.max(s, axis=1, keepdims=True)
        p = jnp.exp2((s - top) * scale).astype(jnp.bfloat16)
        acc = jnp.dot(p, values[:total], preferred_element_type=jnp.float32)
        out = (acc[:, :HEAD] / acc[:, HEAD:]).astype(jnp.bfloat16)
        for n in range(GROUP_HEADS):
            o_ref[span, n * HEAD : (n + 1) * HEAD] = out[n * TILE : (n + 1) * TILE]


def attend(queries, pulled, suffix_pair, page_count):
    tokens, width = queries.shape
    pages = pulled.shape[0]
    block = GROUP_HEADS * HEAD
    return pl.pallas_call(
        functools.partial(attend_kernel, pages),
        out_shape=jax.ShapeDtypeStruct((tokens, width), jnp.bfloat16),
        grid=(KV_HEADS,),
        in_specs=[
            pl.BlockSpec((tokens, block), lambda h: (0, h)),
            pl.BlockSpec((pages, 2, PAGE, HEAD), lambda h: (0, 0, 0, h)),
            pl.BlockSpec((2, tokens, HEAD), lambda h: (0, 0, h)),
            pl.BlockSpec(memory_space=SMEM),
        ],
        out_specs=pl.BlockSpec((tokens, block), lambda h: (0, h)),
        compiler_params=pltpu.CompilerParams(vmem_limit_bytes=48 * 1024 * 1024),
        name="attend",
    )(queries, pulled, suffix_pair, page_count)


def local(queries, suffix_kv, slot_page_cache, holder, page_slots, page_count):
    lane = lax.axis_index("ep")
    slots = lax.dynamic_index_in_dim(page_slots, lane, axis=2, keepdims=False)
    outgoing = pack(holder, slots, slot_page_cache[0, 0])
    arrived = lax.all_to_all(outgoing, "grp", split_axis=0, concat_axis=0, tiled=True)
    forward = select(holder, arrived)
    pulled = lax.all_to_all(forward, "ep", split_axis=0, concat_axis=0, tiled=True)
    return attend(queries[0, 0], pulled, suffix_kv[0, 0], page_count)[None, None]


def solution(mesh):
    return jax.shard_map(
        local,
        mesh=mesh,
        in_specs=(
            P("grp", "ep", None, None),
            P("grp", "ep", None, None, None),
            P("grp", "ep", None, None, None, None),
            P(),
            P(),
            P(),
        ),
        out_specs=P("grp", "ep", None, None),
        check_vma=False,
    )
```

time: 403 us -> 290 us (0.72)
  waiting for transfers between devices: 229 us -> 0 us
  Pallas kernels: 0 us -> 151 us
  blocking collectives: 0 us -> 136 us
  matrix products: 96.9 us -> 0 us
  local copies, waits for them, and re-layouts: 39.2 us -> 1.72 us
  other arithmetic: 19.3 us -> 0 us
  starting transfers between devices: 16.9 us -> 0 us
    all_to_all x2 -> x0, waiting for transfers between devices: 229 us -> none  [the longest x1 185 us: local(): lax.all_to_all(outgoing, 'grp', split_axis=0, concat_axis=0, tiled=True)]
    pallas_call x0 -> x3, Pallas kernels: none -> 151 us  [the longest x1 65.8 us: select(): pl.pallas_call(functools.partial(select_kernel, n_grp, n_ep), out_shape=j...]
    all_to_all x0 -> x2, blocking collectives: none -> 136 us  [the longest x1 71.8 us: local(): lax.all_to_all(outgoing, 'grp', split_axis=0, concat_axis=0, tiled=True)]
    sub x8 -> x0, matrix products: 57.2 us -> none  [one_head(): raised = jnp.where(allowed[None], jnp.exp(scores - top_score), 0.0)]
    dot_general x8 -> x0, matrix products: 39.7 us -> none  [one_head(): jnp.einsum('gst,td->gsd', weights, v_head, preferred_element_type=jnp.flo...]
    gather x2 -> x0, local copies, waits for them, and re-layouts: 17.5 us -> none  [the longest x1 9.72 us: local(): gathered = page_rows[my_slots]]
    select_n x10 -> x0, other arithmetic: 17.2 us -> none  [the longest x1 14 us: local(): jnp.where(owned_here[:, :, None, None, None], gathered, jnp.zeros_like(ga...]
    all_to_all x2 -> x0, starting transfers between devices: 16.9 us -> none  [the longest x1 11.1 us: local(): lax.all_to_all(forward, 'ep', split_axis=0, concat_axis=0, tiled=True)]
  transfers between devices with their start and end apart: 2 -> 0, of which waited for: 2 -> 0; matrix products, arithmetic and copies ran while one was open for 2% -> 0% of each run, Pallas kernels for 0% -> 0%
where the time goes in v1:
time: 290 us; the launch traced here: 289 us
  Pallas kernels  151 us (52%)
  blocking collectives  136 us (47%)
    all_to_all x1, blocking collectives, local(): lax.all_to_all(outgoing, 'grp', split_axis=0, concat_axis=0, tiled=True)  71.8 us
    pallas_call x1, Pallas kernels, select(): pl.pallas_call(functools.partial(select_kernel, n_grp, n_ep), out_shape=j...  65.8 us
    all_to_all x1, blocking collectives, local(): lax.all_to_all(forward, 'ep', split_axis=0, concat_axis=0, tiled=True)  63.9 us
    pallas_call x1, Pallas kernels, pack(): pl.pallas_call(functools.partial(pack_kernel, n_grp, n_ep), out_shape=jax...  60.1 us
    pallas_call x1, Pallas kernels, attend(): pl.pallas_call(functools.partial(attend_kernel, pages), out_shape=jax.Sha...  25.3 us

profile of v1, /device:TPU:32, one launch (start us, length us, event | category | flops | bytes accessed | tf_op | source)
XLA Modules:
  0.0 288.6 jit_solution(13695691863425359465)
XLA Ops:
  0.0 0.0 copy-start
  0.0 0.9 copy-done
  0.9 0.1 constant_dynamic-slice_fusion
  1.0 0.7 copy.8
  1.7 60.1 %pack_pages.1 = bf16[64,2,16,1024]{3,2,1,0:T(8,128)(2,1)} custom-call(s32[8,32]{1,0:T(8,128)} %holder_ref.3, s32[8,32]{1,0:T(8,128)} %bitcast.8, bf16[16,2,16,1024]{3,2,1,0:T(8,128)(2,1)} %bitcast.7), custom_call_target="tpu_custom_call" | custom-call | tf_op jit(solution)/shard_map/pack_pages/pallas_call | solution.py:54
  61.8 71.8 %all_to_all.10.arrived_ref = bf16[64,2,16,1024]{3,2,1,0:T(8,128)(2,1)} all-to-all(bf16[64,2,16,1024]{3,2,1,0:T(8,128)(2,1)} %pack_pages.1), channel_id=1, replica_groups=mesh['grp'=8,'ep'=32] {'grp'}, dimensions={0} | all-to-all | bytes 8388608 | tf_op jit(solution)/shard_map/all_to_all | solution.py:167
  133.6 0.0 copy-start.1
  133.6 0.0 copy-start.2
  133.6 65.8 %select_pages.1 = bf16[32,2,16,1024]{3,2,1,0:T(8,128)(2,1)} custom-call(s32[8,32]{1,0:T(8,128)} %holder_ref.3, bf16[64,2,16,1024]{3,2,1,0:T(8,128)(2,1)} %all_to_all.10.arrived_ref), custom_call_target="tpu_custom_call" | custom-call | tf_op jit(solution)/shard_map/select_pages/pallas_call | solution.py:95
  199.4 63.9 %all_to_all.11.pulled_ref = bf16[32,2,16,1024]{3,2,1,0:T(8,128)(2,1)S(1)} all-to-all(bf16[32,2,16,1024]{3,2,1,0:T(8,128)(2,1)} %select_pages.1), channel_id=1, replica_groups=mesh['grp'=8,'ep'=32] {'ep'}, dimensions={0} | all-to-all | bytes 4194304 | tf_op jit(solution)/shard_map/all_to_all | solution.py:169
  263.3 0.0 copy-done.1
  263.3 0.0 copy-done.2
  263.3 25.3 %attend.1 = bf16[384,5120]{1,0:T(8,128)(2,1)} custom-call(bf16[384,5120]{1,0:T(8,128)(2,1)} %bitcast.6, bf16[32,2,16,1024]{3,2,1,0:T(8,128)(2,1)S(1)} %all_to_all.11.pulled_ref, bf16[2,384,1024]{2,1,0:T(8,128)(2,1)S(1)} %bitcast.5, s32[8,32]{1,0:T(8,128)S(1)} %copy-done.2), custom_call_target="tpu_custom_call" | custom-call | tf_op jit(solution)/shard_map/attend/pallas_call | solution.py:147
Async XLA Ops:
  0.0 0.9 copy-start
  133.6 129.7 %copy-start.1 = (bf16[1,1,2,384,1024]{4,3,2,1,0:T(8,128)(2,1)S(1)}, bf16[1,1,2,384,1024]{4,3,2,1,0:T(8,128)(2,1)}, u32[]{:S(2)}) copy-start(bf16[1,1,2,384,1024]{4,3,2,1,0:T(8,128)(2,1)} %param.7) | copy-start | bytes 4718596
  133.6 129.7 %copy-start.2 = (s32[8,32]{1,0:T(8,128)S(1)}, s32[8,32]{1,0:T(8,128)}, u32[]{:S(2)}) copy-start(s32[8,32]{1,0:T(8,128)} %count_ref.1) | copy-start | bytes 3076

commit v2 on v1

v2 whole, which is shorter than its diff:
```python
import functools
import math

import jax
import jax.numpy as jnp
from jax import lax
from jax.experimental import pallas as pl
from jax.experimental.pallas import tpu as pltpu
from jax.sharding import PartitionSpec as P

HEAD = 128
KV_HEADS = 8
GROUP_HEADS = 5
PAGE = 16
CAP = 8
TILE = 128
SMEM = pltpu.MemorySpace.SMEM
NEG = -1e30
SCALE = math.log2(math.e) / math.sqrt(HEAD)
RING = 4
SHIFTS = [(dy, dx) for dy in range(RING) for dx in range(2)]
CHUNKS = ((0, 5), (5, 3))
ORDER = (1, 2, 3, 4, 5, 6, 7)
TIE = 2
DEPTH = 3
MIB = 1024 * 1024


def target(group, dy, dx):
    return lax.rem(group // 2 + dy, RING) * 2 + lax.rem(group + dx, 2)


def pack_kernel(n_ep, holder_ref, slots_ref, cache_ref, *rest):
    n = len(SHIFTS)
    outs = [rest[c * n : (c + 1) * n] for c in range(len(CHUNKS))]
    list_ref, held, sem, out_sem = rest[len(CHUNKS) * n :]
    me = lax.axis_index("grp")
    load = pltpu.make_async_copy(cache_ref, held, sem)
    load.start()

    def copy(c, s, slot, k):
        first, heads = CHUNKS[c]
        part = held.at[slot, :, :, pl.ds(first * HEAD, heads * HEAD)]
        return pltpu.make_async_copy(part, outs[c][s].at[k], out_sem.at[c, s, k])

    counts = []
    for s, (dy, dx) in enumerate(SHIFTS):
        g = target(me, dy, dx)

        count = jnp.int32(0)
        for base in range(0, n_ep, 8):
            span = range(base, min(base + 8, n_ep))
            mine = [(holder_ref[g, e] == me).astype(jnp.int32) for e in span]
            slot = [slots_ref[g, e] for e in span]
            for one, held_in in zip(mine, slot):
                list_ref[s, count] = held_in
                count = count + one
        counts.append(count)
        if s == 0:
            load.wait()

        def send(k, carry, s=s):
            for c in range(len(CHUNKS)):
                copy(c, s, list_ref[s, k], k).start()
            return carry

        lax.fori_loop(0, counts[s], send, 0)
    for s, count in enumerate(counts):

        def drain(k, carry, s=s):
            for c in range(len(CHUNKS)):
                copy(c, s, 0, k).wait()
            return carry

        lax.fori_loop(0, count, drain, 0)


def pack(holder, slots, cache):
    n_slots, pair, page, _ = cache.shape
    n = len(SHIFTS)
    outs = pl.pallas_call(
        functools.partial(pack_kernel, holder.shape[1]),
        out_shape=[
            jax.ShapeDtypeStruct((CAP, pair, page, heads * HEAD), cache.dtype) for _, heads in CHUNKS for _ in SHIFTS
        ],
        in_specs=[
            pl.BlockSpec(memory_space=SMEM),
            pl.BlockSpec(memory_space=SMEM),
            pl.BlockSpec(memory_space=pl.ANY),
        ],
        out_specs=[pl.BlockSpec(memory_space=pl.ANY)] * (n * len(CHUNKS)),
        scratch_shapes=[
            pltpu.SMEM((n, 2 * CAP), jnp.int32),
            pltpu.VMEM(cache.shape, cache.dtype),
            pltpu.SemaphoreType.DMA,
            pltpu.SemaphoreType.DMA((len(CHUNKS), n, CAP)),
        ],
        compiler_params=pltpu.CompilerParams(vmem_limit_bytes=63 * MIB),
        cost_estimate=pl.CostEstimate(flops=0, bytes_accessed=6 * MIB, transcendentals=0),
        name="pack_pages",
    )(holder, slots, cache)
    return [outs[c * n : (c + 1) * n] for c in range(len(CHUNKS))]


def select_kernel(n_ep, holder_ref, *rest):
    arrived, (out_ref, count_ref, held, sem, out_sem) = rest[: len(SHIFTS)], rest[len(SHIFTS) :]
    me = lax.axis_index("grp")
    loads = [pltpu.make_async_copy(arrived[s], held.at[s], sem.at[s]) for s in range(len(SHIFTS))]
    for load in loads:
        load.start()
    for s in range(len(SHIFTS)):
        count_ref[s] = 0
    for load in loads:
        load.wait()

    def request(e, carry):
        h = holder_ref[me, e]
        s = lax.rem(me // 2 - h // 2 + RING, RING) * 2 + lax.rem(me + h, 2)
        k = count_ref[s]
        pltpu.make_async_copy(held.at[s, k], out_ref.at[e], out_sem.at[e]).start()
        count_ref[s] = k + 1
        return carry

    lax.fori_loop(0, n_ep, request, 0, unroll=8)

    def drain(e, carry):
        pltpu.make_async_copy(held.at[0, 0], out_ref.at[e], out_sem.at[e]).wait()
        return carry

    lax.fori_loop(0, n_ep, drain, 0, unroll=8)


def select(holder, arrived):
    n_ep = holder.shape[1]
    one = arrived[0].shape[1:]
    dtype = arrived[0].dtype
    return pl.pallas_call(
        functools.partial(select_kernel, n_ep),
        out_shape=jax.ShapeDtypeStruct((n_ep,) + one, dtype),
        in_specs=[pl.BlockSpec(memory_space=SMEM)] + [pl.BlockSpec(memory_space=pl.ANY)] * len(SHIFTS),
        out_specs=pl.BlockSpec(memory_space=pl.ANY),
        scratch_shapes=[
            pltpu.SMEM((len(SHIFTS),), jnp.int32),
            pltpu.VMEM((len(SHIFTS), CAP) + one, dtype),
            pltpu.SemaphoreType.DMA((len(SHIFTS),)),
            pltpu.SemaphoreType.DMA((n_ep,)),
        ],
        compiler_params=pltpu.CompilerParams(vmem_limit_bytes=63 * MIB),
        cost_estimate=pl.CostEstimate(flops=0, bytes_accessed=6 * MIB, transcendentals=0),
        name="select_pages",
    )(holder, *arrived)


def triangle():
    return lax.broadcasted_iota(jnp.int32, (TILE, TILE), 0) >= lax.broadcasted_iota(jnp.int32, (TILE, TILE), 1)


def prefix_pair(pulled_ref, valid):
    prefix = pulled_ref.shape[0] * PAGE
    ok = lax.broadcasted_iota(jnp.int32, (prefix, HEAD), 0) < valid
    keys = pulled_ref[:, 0].reshape(prefix, HEAD).astype(jnp.float32)
    keys = jnp.where(ok, keys, keys[0:1, :]).astype(jnp.bfloat16)
    values = pulled_ref[:, 1].reshape(prefix, HEAD).astype(jnp.float32)
    values = jnp.where(ok, values, 0.0).astype(jnp.bfloat16)
    ones = jnp.where(ok, 1.0, 0.0).astype(jnp.bfloat16)
    return keys, jnp.concatenate([values, ones], axis=1)


def suffix_pair_of(suffix_ref):
    return suffix_ref[0], jnp.concatenate([suffix_ref[1], jnp.ones(suffix_ref.shape[1:], jnp.bfloat16)], axis=1)


def attend_kernel(q_ref, pulled_ref, suffix_ref, count_ref, *rest):
    o_ref = rest[-1]
    valid = count_ref[lax.axis_index("grp"), lax.axis_index("ep")] * PAGE
    k_pre, v_pre = prefix_pair(pulled_ref, valid)
    k_suf, v_suf = suffix_pair_of(suffix_ref)
    keys = jnp.concatenate([k_pre, k_suf], axis=0)
    values = jnp.concatenate([v_pre, v_suf], axis=0)
    tri = triangle()
    tiles = [(i, n) for i in range(q_ref.shape[0] // TILE) for n in range(GROUP_HEADS)]

    def place(tile):
        i, n = tile
        return slice(i * TILE, (i + 1) * TILE), slice(n * HEAD, (n + 1) * HEAD)

    def total(tile):
        return k_pre.shape[0] + (tile[0] + 1) * TILE

    def score(tile):
        q = q_ref[place(tile)]
        return lax.dot_general(q, keys[: total(tile)], (((1,), (1,)), ((), ())), preferred_element_type=jnp.float32)

    def weigh(tile, s):
        end = total(tile)
        s = jnp.concatenate([s[:, : end - TILE], jnp.where(tri, s[:, end - TILE :], NEG)], axis=1)
        top = jnp.max(s, axis=1, keepdims=True)
        return jnp.exp2((s - top) * SCALE).astype(jnp.bfloat16)

    def mix(tile, p):
        return jnp.dot(p, values[: total(tile)], preferred_element_type=jnp.float32)

    scores, weights, mixed = {}, {}, {}
    for t in range(len(tiles) + 3 * DEPTH):
        if t < len(tiles):
            scores[t] = score(tiles[t])
        u = t - DEPTH
        if 0 <= u < len(tiles):
            weights[u] = weigh(tiles[u], scores.pop(u))
        u -= DEPTH
        if 0 <= u < len(tiles):
            mixed[u] = mix(tiles[u], weights.pop(u))
        u -= DEPTH
        if 0 <= u < len(tiles):
            acc = mixed.pop(u)
            o_ref[place(tiles[u])] = (acc[:, :HEAD] / acc[:, HEAD:]).astype(jnp.bfloat16)


def cost(heads, keys):
    work = heads * GROUP_HEADS * 384 * keys
    return pl.CostEstimate(flops=4 * HEAD * work, bytes_accessed=heads * MIB * 3 // 2, transcendentals=work)


def attend(chunk, queries, pulled, suffix, page_count, so_far):
    first, heads = chunk
    tokens, width = queries.shape
    pages = pulled.shape[0]
    block = GROUP_HEADS * HEAD
    operands = [queries, pulled, suffix, page_count]
    in_specs = [
        pl.BlockSpec((tokens, block), lambda h: (0, first + h)),
        pl.BlockSpec((pages, 2, PAGE, HEAD), lambda h: (0, 0, 0, h)),
        pl.BlockSpec((2, tokens, HEAD), lambda h: (0, 0, first + h)),
        pl.BlockSpec(memory_space=SMEM),
    ]
    aliases = {}
    if so_far is not None:
        aliases = {len(operands): 0}
        operands.append(so_far)
        in_specs.append(pl.BlockSpec(memory_space=pl.ANY))
    return pl.pallas_call(
        attend_kernel,
        out_shape=jax.ShapeDtypeStruct((tokens, width), jnp.bfloat16),
        grid=(heads,),
        in_specs=in_specs,
        out_specs=pl.BlockSpec((tokens, block), lambda h: (0, first + h)),
        input_output_aliases=aliases,
        compiler_params=pltpu.CompilerParams(vmem_limit_bytes=63 * MIB),
        cost_estimate=cost(heads, 768),
        name="attend",
    )(*operands)


def shift(page, dy, dx):
    pairs = [(y * 2 + x, (y + dy) % RING * 2 + (x + dx) % 2) for y in range(RING) for x in range(2)]
    return lax.ppermute(page, "grp", pairs)


def exchange(pages):
    return lax.all_to_all(pages, "ep", split_axis=0, concat_axis=0, tiled=True)


def local(queries, suffix_kv, slot_page_cache, holder, page_slots, page_count):
    lane = lax.axis_index("ep")
    slots = lax.dynamic_index_in_dim(page_slots, lane, axis=2, keepdims=False)
    q, suffix = queries[0, 0], suffix_kv[0, 0]
    arrived = []
    for pages in pack(holder, slots, slot_page_cache[0, 0]):
        got = {0: pages[0]}
        for s in ORDER:
            got[s] = shift(pages[s], *SHIFTS[s])
        arrived.append([got[s] for s in range(len(SHIFTS))])
    pulled = []
    for c in range(len(CHUNKS)):
        forward = select(holder, arrived[c])
        if TIE and c + 1 < len(CHUNKS):
            tied = [arrived[c + 1][s] for s in ORDER[:TIE]]
            forward, tied = lax.optimization_barrier((forward, tied))
            for s, t in zip(ORDER[:TIE], tied):
                arrived[c + 1][s] = t
        pulled.append(exchange(forward))
    out = None
    for c, chunk in enumerate(CHUNKS):
        out = attend(chunk, q, pulled[c], suffix, page_count, out)
    return out[None, None]


def solution(mesh):
    return jax.shard_map(
        local,
        mesh=mesh,
        in_specs=(
            P("grp", "ep", None, None),
            P("grp", "ep", None, None, None),
            P("grp", "ep", None, None, None, None),
            P(),
            P(),
            P(),
        ),
        out_specs=P("grp", "ep", None, None),
        check_vma=False,
    )
```

time: 290 us -> 138 us (0.48)
  blocking collectives: 136 us -> 0 us
  Pallas kernels: 151 us -> 34.1 us
  waiting for transfers between devices: 0 us -> 53.9 us
  starting transfers between devices: 0 us -> 47.9 us
    all_to_all x2 -> x0, blocking collectives: 136 us -> none  [the longest x1 71.8 us: local(): lax.all_to_all(outgoing, 'grp', split_axis=0, concat_axis=0, tiled=True)]
    pallas_call x3 -> x5, Pallas kernels: 151 us -> 34.1 us  [the longest x2 22.2 us: attend(): pl.pallas_call(attend_kernel, out_shape=jax.ShapeDtypeStruct((tokens, wid...]
    ppermute x0 -> x14, waiting for transfers between devices: none -> 40.9 us  [shift(): return lax.ppermute(page, 'grp', pairs)]
    ppermute x0 -> x14, starting transfers between devices: none -> 28.2 us  [shift(): return lax.ppermute(page, 'grp', pairs)]
    all_to_all x0 -> x2, starting transfers between devices: none -> 19.7 us  [exchange(): return lax.all_to_all(pages, 'ep', split_axis=0, concat_axis=0, tiled=True)]
    all_to_all x0 -> x2, waiting for transfers between devices: none -> 13 us  [exchange(): return lax.all_to_all(pages, 'ep', split_axis=0, concat_axis=0, tiled=True)]
  transfers between devices with their start and end apart: 0 -> 16, of which waited for: 0 -> 11; matrix products, arithmetic and copies ran while one was open for 0% -> 0% of each run, Pallas kernels for 0% -> 15%
where the time goes in v2:
time: 138 us; the launch traced here: 139 us
  waiting for transfers between devices  53.9 us (39%)
  starting transfers between devices  47.9 us (35%)
  Pallas kernels  34.1 us (25%)
  local copies, waits for them, and re-layouts  2.61 us (2%)
    ppermute x14, waiting for transfers between devices, shift(): return lax.ppermute(page, 'grp', pairs)  40.9 us
    ppermute x14, starting transfers between devices, shift(): return lax.ppermute(page, 'grp', pairs)  28.2 us
    pallas_call x2, Pallas kernels, attend(): pl.pallas_call(attend_kernel, out_shape=jax.ShapeDtypeStruct((tokens, wid...  22.2 us
    all_to_all x2, starting transfers between devices, exchange(): return lax.all_to_all(pages, 'ep', split_axis=0, concat_axis=0, tiled=True)  19.7 us
    all_to_all x2, waiting for transfers between devices, exchange(): return lax.all_to_all(pages, 'ep', split_axis=0, concat_axis=0, tiled=True)  13 us
    pallas_call x2, Pallas kernels, select(): pl.pallas_call(functools.partial(select_kernel, n_ep), out_shape=jax.Shap...  7.19 us
    pallas_call x1, Pallas kernels, pack(): pl.pallas_call(functools.partial(pack_kernel, holder.shape[1]), out_shape...  4.74 us
  transfers between devices with their start and end apart: 16, of which 11 were waited for; matrix products, arithmetic and copies ran while one was open for 0% of the time, Pallas kernels for 15%

profile of v2, /device:TPU:32, one launch (start us, length us, event | category | flops | bytes accessed | tf_op | source)
XLA Modules:
  0.0 138.6 jit_solution(14493212942282123027)
XLA Ops:
  0.0 0.0 copy-start
  0.0 0.9 copy-done
  0.9 0.1 constant_dynamic-slice_fusion
  1.0 0.7 copy.9
  1.7 4.7 %pack_pages.1 = (bf16[8,2,16,640]{3,2,1,0:T(8,128)(2,1)}, bf16[8,2,16,640]{3,2,1,0:T(8,128)(2,1)}, bf16[8,2,16,640]{3,2,1,0:T(8,128)(2,1)}, bf16[8,2,16,640]{3,2...) custom-call(s32[8,32]{1,0:T(8,128)} %holder_ref.5, ...), custom_call_target="tpu_custom_call" | custom-call | bytes 6291456 | tf_op jit(solution)/shard_map/pack_pages/pallas_call | solution.py:81
  6.5 1.3 collective-permute-start
  7.7 1.7 %collective-permute-start.1 = (bf16[8,2,16,640]{3,2,1,0:T(8,128)(2,1)}, bf16[8,2,16,640]{3,2,1,0:T(8,128)(2,1)S(1)}, u32[]{:S(2)}, u32[]{:S(2)}) collective-permute-start(bf16[8,2,16,640]{3,2,1,0:T(8,128)(2,1)} %get-tuple-element.27), channel_id=1, source_target_pairs={{0,64},{32,96},{64,128},{96,160},{128,192},{160,224},{192,0},{224,... | collective-permute-start | bytes 983048 | tf_op jit(solution)/shard_map/ppermute | solution.py:256
  9.5 1.9 %collective-permute-start.2 = (bf16[8,2,16,640]{3,2,1,0:T(8,128)(2,1)}, bf16[8,2,16,640]{3,2,1,0:T(8,128)(2,1)}, u32[]{:S(2)}, u32[]{:S(2)}) collective-permute-start(bf16[8,2,16,640]{3,2,1,0:T(8,128)(2,1)} %get-tuple-element.28), channel_id=1, source_target_pairs={{0,96},{32,64},{64,160},{96,128},{128,224},{160,192},{192,32},{224... | collective-permute-start | bytes 983048 | tf_op jit(solution)/shard_map/ppermute | solution.py:256
  11.4 1.3 collective-permute-start.3
  12.7 2.9 %collective-permute-start.4 = (bf16[8,2,16,640]{3,2,1,0:T(8,128)(2,1)}, bf16[8,2,16,640]{3,2,1,0:T(8,128)(2,1)}, u32[]{:S(2)}, u32[]{:S(2)}) collective-permute-start(bf16[8,2,16,640]{3,2,1,0:T(8,128)(2,1)} %get-tuple-element.30), channel_id=1, source_target_pairs={{0,160},{32,128},{64,224},{96,192},{128,32},{160,0},{192,96},{224,... | collective-permute-start | bytes 983048 | tf_op jit(solution)/shard_map/ppermute | solution.py:256
  15.6 1.7 %collective-permute-done.rest_1_ = bf16[8,2,16,640]{3,2,1,0:T(8,128)(2,1)S(1)} collective-permute-done((bf16[8,2,16,640]{3,2,1,0:T(8,128)(2,1)}, bf16[8,2,16,640]{3,2,1,0:T(8,128)(2,1)S(1)}, u32[]{:S(2)}, u32[]{:S(2)}) %collective-permute-start) | collective-permute-done | bytes 327712 | tf_op jit(solution)/shard_map/ppermute | solution.py:256
  17.4 3.1 %collective-permute-start.5 = (bf16[8,2,16,640]{3,2,1,0:T(8,128)(2,1)}, bf16[8,2,16,640]{3,2,1,0:T(8,128)(2,1)}, u32[]{:S(2)}, u32[]{:S(2)}) collective-permute-start(bf16[8,2,16,640]{3,2,1,0:T(8,128)(2,1)} %get-tuple-element.31), channel_id=1, source_target_pairs={{0,192},{32,224},{64,0},{96,32},{128,64},{160,96},{192,128},{224,1... | collective-permute-start | bytes 983048 | tf_op jit(solution)/shard_map/ppermute | solution.py:256
  20.5 11.7 %collective-permute-done.1.rest_2_ = bf16[8,2,16,640]{3,2,1,0:T(8,128)(2,1)S(1)} collective-permute-done((bf16[8,2,16,640]{3,2,1,0:T(8,128)(2,1)}, bf16[8,2,16,640]{3,2,1,0:T(8,128)(2,1)S(1)}, u32[]{:S(2)}, u32[]{:S(2)}) %collective-permute-start.1) | collective-permute-done | bytes 327712 | tf_op jit(solution)/shard_map/ppermute | solution.py:256
  32.2 3.8 %collective-permute-start.6 = (bf16[8,2,16,640]{3,2,1,0:T(8,128)(2,1)}, bf16[8,2,16,640]{3,2,1,0:T(8,128)(2,1)}, u32[]{:S(2)}, u32[]{:S(2)}) collective-permute-start(bf16[8,2,16,640]{3,2,1,0:T(8,128)(2,1)} %get-tuple-element.32), channel_id=1, source_target_pairs={{0,224},{32,192},{64,32},{96,0},{128,96},{160,64},{192,160},{224,1... | collective-permute-start | bytes 983048 | tf_op jit(solution)/shard_map/ppermute | solution.py:256
  36.0 0.0 collective-permute-done.2.rest_3_
  36.0 1.3 collective-permute-start.7
  37.4 3.6 %collective-permute-done.3.rest_4_ = bf16[8,2,16,640]{3,2,1,0:T(8,128)(2,1)} collective-permute-done((bf16[8,2,16,640]{3,2,1,0:T(8,128)(2,1)}, bf16[8,2,16,640]{3,2,1,0:T(8,128)(2,1)}, u32[]{:S(2)}, u32[]{:S(2)}) %collective-permute-start.3) | collective-permute-done | bytes 327712 | tf_op jit(solution)/shard_map/ppermute | solution.py:256
  41.0 0.0 collective-permute-start.8
  41.0 0.0 collective-permute-done.4.rest_5_
  41.0 0.8 collective-permute-done.5.rest_6_
  41.8 0.0 collective-permute-done.6.rest_7_
  41.8 0.0 copy-done.2
  41.8 0.0 copy-done.3
  41.9 3.8 %select_pages.2 = bf16[32,2,16,640]{3,2,1,0:T(8,128)(2,1)} custom-call(s32[8,32]{1,0:T(8,128)} %holder_ref.5, bf16[8,2,16,640]{3,2,1,0:T(8,128)(2,1)} %get-tuple-element.25.rest_0_, bf16[8,2,16,640]{3,2,1,0:T(8,128)(2,1)} %copy-done.2, bf16[8,2,16,640]{3,2,1,0:T(8,128)(2,1)} %copy-done.3, bf16[8,2,16,640]{3,2,1,0:T(8,128)(2,1)} %collective-permute-done.2.rest_3_, ...), custom_call_target="tpu_custom_call" | custom-call | bytes 6291456 | tf_op jit(solution)/shard_map/select_pages/pallas_call | solution.py:137
  45.6 0.0 collective-permute-done.7.rest_1_
  45.6 0.0 copy-start.4
  45.7 2.5 %collective-permute-done.8.rest_2_ = bf16[8,2,16,384]{3,2,1,0:T(8,128)(2,1)} collective-permute-done((bf16[8,2,16,384]{3,2,1,0:T(8,128)(2,1)}, bf16[8,2,16,384]{3,2,1,0:T(8,128)(2,1)}, u32[]{:S(2)}, u32[]{:S(2)}) %collective-permute-start.8) | collective-permute-done | bytes 196640 | tf_op jit(solution)/shard_map/ppermute | solution.py:256
  48.2 10.9 %all-to-all-start.1 = ((bf16[32,2,16,640]{3,2,1,0:T(8,128)(2,1)}), bf16[32,2,16,640]{3,2,1,0:T(8,128)(2,1)}, u32[]{:S(2)}, u32[]{:S(2)}) async-start(bf16[32,2,16,640]{3,2,1,0:T(8,128)(2,1)} %select_pages.2), calls=%async_computation.1 | async-start | bytes 2621440 | tf_op jit(solution)/shard_map/all_to_all | solution.py:260
  59.1 3.0 %collective-permute-start.9 = (bf16[8,2,16,384]{3,2,1,0:T(8,128)(2,1)}, bf16[8,2,16,384]{3,2,1,0:T(8,128)(2,1)S(1)}, u32[]{:S(2)}, u32[]{:S(2)}) collective-permute-start(bf16[8,2,16,384]{3,2,1,0:T(8,128)(2,1)} %get-tuple-element.37), channel_id=1, source_target_pairs={{0,96},{32,64},{64,160},{96,128},{128,224},{160,192},{192,32},{224... | collective-permute-start | bytes 589832 | tf_op jit(solution)/shard_map/ppermute | solution.py:256
  62.2 2.8 %collective-permute-start.10 = (bf16[8,2,16,384]{3,2,1,0:T(8,128)(2,1)}, bf16[8,2,16,384]{3,2,1,0:T(8,128)(2,1)S(1)}, u32[]{:S(2)}, u32[]{:S(2)}) collective-permute-start(bf16[8,2,16,384]{3,2,1,0:T(8,128)(2,1)} %get-tuple-element.38), channel_id=1, source_target_pairs={{0,128},{32,160},{64,192},{96,224},{128,0},{160,32},{192,64},{224,... | collective-permute-start | bytes 589832 | tf_op jit(solution)/shard_map/ppermute | solution.py:256
  64.9 0.0 collective-permute-start.11
  64.9 3.4 %collective-permute-start.12 = (bf16[8,2,16,384]{3,2,1,0:T(8,128)(2,1)}, bf16[8,2,16,384]{3,2,1,0:T(8,128)(2,1)}, u32[]{:S(2)}, u32[]{:S(2)}) collective-permute-start(bf16[8,2,16,384]{3,2,1,0:T(8,128)(2,1)} %get-tuple-element.40), channel_id=1, source_target_pairs={{0,192},{32,224},{64,0},{96,32},{128,64},{160,96},{192,128},{224,1... | collective-permute-start | bytes 589832 | tf_op jit(solution)/shard_map/ppermute | solution.py:256
  68.4 1.6 %collective-permute-start.13 = (bf16[8,2,16,384]{3,2,1,0:T(8,128)(2,1)}, bf16[8,2,16,384]{3,2,1,0:T(8,128)(2,1)}, u32[]{:S(2)}, u32[]{:S(2)}) collective-permute-start(bf16[8,2,16,384]{3,2,1,0:T(8,128)(2,1)} %get-tuple-element.41), channel_id=1, source_target_pairs={{0,224},{32,192},{64,32},{96,0},{128,96},{160,64},{192,160},{224,1... | collective-permute-start | bytes 589832 | tf_op jit(solution)/shard_map/ppermute | solution.py:256
  69.9 3.3 %collective-permute-done.9.rest_3_ = bf16[8,2,16,384]{3,2,1,0:T(8,128)(2,1)S(1)} collective-permute-done((bf16[8,2,16,384]{3,2,1,0:T(8,128)(2,1)}, bf16[8,2,16,384]{3,2,1,0:T(8,128)(2,1)S(1)}, u32[]{:S(2)}, u32[]{:S(2)}) %collective-permute-start.9) | collective-permute-done | bytes 196640 | tf_op jit(solution)/shard_map/ppermute | solution.py:256
  73.2 5.0 %collective-permute-done.10.rest_4_ = bf16[8,2,16,384]{3,2,1,0:T(8,128)(2,1)S(1)} collective-permute-done((bf16[8,2,16,384]{3,2,1,0:T(8,128)(2,1)}, bf16[8,2,16,384]{3,2,1,0:T(8,128)(2,1)S(1)}, u32[]{:S(2)}, u32[]{:S(2)}) %collective-permute-start.10) | collective-permute-done | bytes 196640 | tf_op jit(solution)/shard_map/ppermute | solution.py:256
  78.2 2.9 %collective-permute-done.11.rest_5_ = bf16[8,2,16,384]{3,2,1,0:T(8,128)(2,1)S(1)} collective-permute-done((bf16[8,2,16,384]{3,2,1,0:T(8,128)(2,1)}, bf16[8,2,16,384]{3,2,1,0:T(8,128)(2,1)S(1)}, u32[]{:S(2)}, u32[]{:S(2)}) %collective-permute-start.11) | collective-permute-done | bytes 196640 | tf_op jit(solution)/shard_map/ppermute | solution.py:256
  81.1 0.0 collective-permute-done.12.rest_6_
  81.1 9.3 %collective-permute-done.13.rest_7_ = bf16[8,2,16,384]{3,2,1,0:T(8,128)(2,1)} collective-permute-done((bf16[8,2,16,384]{3,2,1,0:T(8,128)(2,1)}, bf16[8,2,16,384]{3,2,1,0:T(8,128)(2,1)}, u32[]{:S(2)}, u32[]{:S(2)}) %collective-permute-start.13) | collective-permute-done | bytes 196640 | tf_op jit(solution)/shard_map/ppermute | solution.py:256
  90.3 0.0 copy-done.4
  90.3 0.0 copy-done.5
  90.3 0.0 copy-done.6
  90.4 3.4 %select_pages.3 = bf16[32,2,16,384]{3,2,1,0:T(8,128)(2,1)} custom-call(s32[8,32]{1,0:T(8,128)} %holder_ref.5, bf16[8,2,16,384]{3,2,1,0:T(8,128)(2,1)} %get-tuple-element.24.rest_0_, bf16[8,2,16,384]{3,2,1,0:T(8,128)(2,1)} %copy-done.4, bf16[8,2,16,384]{3,2,1,0:T(8,128)(2,1)} %collective-permute-done.8.rest_2_, bf16[8,2,16,384]{3,2,1,0:T(8,128)(2,1)} %copy-done.5, ...), custom_call_target="tpu_custom_call" | custom-call | bytes 6291456 | tf_op jit(solution)/shard_map/select_pages/pallas_call | solution.py:137
  93.8 1.5 %all-to-all-done.1.pulled_ref = bf16[32,2,16,640]{3,2,1,0:T(8,128)(2,1)} async-done(((bf16[32,2,16,640]{3,2,1,0:T(8,128)(2,1)}), bf16[32,2,16,640]{3,2,1,0:T(8,128)(2,1)}, u32[]{:S(2)}, u32[]{:S(2)}) %all-to-all-start.1) | async-done | bytes 1310752 | tf_op jit(solution)/shard_map/all_to_all | solution.py:260
  95.3 8.7 %all-to-all-start = ((bf16[32,2,16,384]{3,2,1,0:T(8,128)(2,1)}), bf16[32,2,16,384]{3,2,1,0:T(8,128)(2,1)S(1)}, u32[]{:S(2)}, u32[]{:S(2)}) async-start(bf16[32,2,16,384]{3,2,1,0:T(8,128)(2,1)} %select_pages.3), calls=%async_computation | async-start | bytes 1572864 | tf_op jit(solution)/shard_map/all_to_all | solution.py:260
  104.0 13.4 %attend.2.rest_0_ = bf16[384,5120]{1,0:T(8,128)(2,1)} custom-call(bf16[384,5120]{1,0:T(8,128)(2,1)} %bitcast.5, bf16[32,2,16,640]{3,2,1,0:T(8,128)(2,1)} %all-to-all-done.1.pulled_ref, bf16[2,384,1024]{2,1,0:T(8,128)(2,1)} %bitcast.7, s32[8,32]{1,0:T(8,128)} %count_ref.3), custom_call_target="tpu_custom_call" | custom-call | flops 3774873600 | bytes 7864320 | tf_op jit(solution)/shard_map/attend/pallas_call | solution.py:241
  117.4 11.5 %all-to-all-done.pulled_ref = bf16[32,2,16,384]{3,2,1,0:T(8,128)(2,1)S(1)} async-done(((bf16[32,2,16,384]{3,2,1,0:T(8,128)(2,1)}), bf16[32,2,16,384]{3,2,1,0:T(8,128)(2,1)S(1)}, u32[]{:S(2)}, u32[]{:S(2)}) %all-to-all-start) | async-done | bytes 786464 | tf_op jit(solution)/shard_map/all_to_all | solution.py:260
  128.9 0.9 copy-done.1
  129.8 8.8 %attend.3 = bf16[384,5120]{1,0:T(8,128)(2,1)} custom-call(bf16[384,5120]{1,0:T(8,128)(2,1)} %bitcast.6, bf16[32,2,16,384]{3,2,1,0:T(8,128)(2,1)} %copy-done.1, bf16[2,384,1024]{2,1,0:T(8,128)(2,1)} %bitcast.8, s32[8,32]{1,0:T(8,128)} %count_ref.3, bf16[384,5120]{1,0:T(8,128)(2,1)} %attend.2.rest_0_), custom_call_target="tpu_custom_call", output_to_operand_aliasing={{}: (4, {})} | custom-call | flops 2264924160 | bytes 4718592 | tf_op jit(solution)/shard_map/attend/pallas_call | solution.py:241
  (7 shorter events, 0.0 us)
Async XLA Ops:
  0.0 0.9 copy-start
  6.5 10.9 %collective-permute-start = (bf16[8,2,16,640]{3,2,1,0:T(8,128)(2,1)}, bf16[8,2,16,640]{3,2,1,0:T(8,128)(2,1)S(1)}, u32[]{:S(2)}, u32[]{:S(2)}) collective-permute-start(bf16[8,2,16,640]{3,2,1,0:T(8,128)(2,1)} %get-tuple-element.26), channel_id=1, source_target_pairs={{0,32},{32,0},{64,96},{96,64},{128,160},{160,128},{192,224},{224,1... | collective-permute-start | bytes 983048 | tf_op jit(solution)/shard_map/ppermute | solution.py:256
  7.7 24.5 %collective-permute-start.1 = (bf16[8,2,16,640]{3,2,1,0:T(8,128)(2,1)}, bf16[8,2,16,640]{3,2,1,0:T(8,128)(2,1)S(1)}, u32[]{:S(2)}, u32[]{:S(2)}) collective-permute-start(bf16[8,2,16,640]{3,2,1,0:T(8,128)(2,1)} %get-tuple-element.27), channel_id=1, source_target_pairs={{0,64},{32,96},{64,128},{96,160},{128,192},{160,224},{192,0},{224,... | collective-permute-start | bytes 983048 | tf_op jit(solution)/shard_map/ppermute | solution.py:256
  9.5 26.5 %collective-permute-start.2 = (bf16[8,2,16,640]{3,2,1,0:T(8,128)(2,1)}, bf16[8,2,16,640]{3,2,1,0:T(8,128)(2,1)}, u32[]{:S(2)}, u32[]{:S(2)}) collective-permute-start(bf16[8,2,16,640]{3,2,1,0:T(8,128)(2,1)} %get-tuple-element.28), channel_id=1, source_target_pairs={{0,96},{32,64},{64,160},{96,128},{128,224},{160,192},{192,32},{224... | collective-permute-start | bytes 983048 | tf_op jit(solution)/shard_map/ppermute | solution.py:256
  11.4 29.6 %collective-permute-start.3 = (bf16[8,2,16,640]{3,2,1,0:T(8,128)(2,1)}, bf16[8,2,16,640]{3,2,1,0:T(8,128)(2,1)}, u32[]{:S(2)}, u32[]{:S(2)}) collective-permute-start(bf16[8,2,16,640]{3,2,1,0:T(8,128)(2,1)} %get-tuple-element.29), channel_id=1, source_target_pairs={{0,128},{32,160},{64,192},{96,224},{128,0},{160,32},{192,64},{224,... | collective-permute-start | bytes 983048 | tf_op jit(solution)/shard_map/ppermute | solution.py:256
  12.7 28.3 %collective-permute-start.4 = (bf16[8,2,16,640]{3,2,1,0:T(8,128)(2,1)}, bf16[8,2,16,640]{3,2,1,0:T(8,128)(2,1)}, u32[]{:S(2)}, u32[]{:S(2)}) collective-permute-start(bf16[8,2,16,640]{3,2,1,0:T(8,128)(2,1)} %get-tuple-element.30), channel_id=1, source_target_pairs={{0,160},{32,128},{64,224},{96,192},{128,32},{160,0},{192,96},{224,... | collective-permute-start | bytes 983048 | tf_op jit(solution)/shard_map/ppermute | solution.py:256
  17.4 24.5 %copy-start.2 = (bf16[8,2,16,640]{3,2,1,0:T(8,128)(2,1)}, bf16[8,2,16,640]{3,2,1,0:T(8,128)(2,1)S(1)}, u32[]{:S(2)}) copy-start(bf16[8,2,16,640]{3,2,1,0:T(8,128)(2,1)S(1)} %collective-permute-done.rest_1_) | copy-start | bytes 983044
  17.4 24.5 %collective-permute-start.5 = (bf16[8,2,16,640]{3,2,1,0:T(8,128)(2,1)}, bf16[8,2,16,640]{3,2,1,0:T(8,128)(2,1)}, u32[]{:S(2)}, u32[]{:S(2)}) collective-permute-start(bf16[8,2,16,640]{3,2,1,0:T(8,128)(2,1)} %get-tuple-element.31), channel_id=1, source_target_pairs={{0,192},{32,224},{64,0},{96,32},{128,64},{160,96},{192,128},{224,1... | collective-permute-start | bytes 983048 | tf_op jit(solution)/shard_map/ppermute | solution.py:256
  32.2 9.7 %copy-start.3 = (bf16[8,2,16,640]{3,2,1,0:T(8,128)(2,1)}, bf16[8,2,16,640]{3,2,1,0:T(8,128)(2,1)S(1)}, u32[]{:S(2)}) copy-start(bf16[8,2,16,640]{3,2,1,0:T(8,128)(2,1)S(1)} %collective-permute-done.1.rest_2_) | copy-start | bytes 983044
  32.2 9.7 %collective-permute-start.6 = (bf16[8,2,16,640]{3,2,1,0:T(8,128)(2,1)}, bf16[8,2,16,640]{3,2,1,0:T(8,128)(2,1)}, u32[]{:S(2)}, u32[]{:S(2)}) collective-permute-start(bf16[8,2,16,640]{3,2,1,0:T(8,128)(2,1)} %get-tuple-element.32), channel_id=1, source_target_pairs={{0,224},{32,192},{64,32},{96,0},{128,96},{160,64},{192,160},{224,1... | collective-permute-start | bytes 983048 | tf_op jit(solution)/shard_map/ppermute | solution.py:256
  36.0 9.6 %collective-permute-start.7 = (bf16[8,2,16,384]{3,2,1,0:T(8,128)(2,1)}, bf16[8,2,16,384]{3,2,1,0:T(8,128)(2,1)S(1)}, u32[]{:S(2)}, u32[]{:S(2)}) collective-permute-start(bf16[8,2,16,384]{3,2,1,0:T(8,128)(2,1)} %get-tuple-element.33), channel_id=1, source_target_pairs={{0,32},{32,0},{64,96},{96,64},{128,160},{160,128},{192,224},{224,1... | collective-permute-start | bytes 589832 | tf_op jit(solution)/shard_map/ppermute | solution.py:256
  41.0 7.2 %collective-permute-start.8 = (bf16[8,2,16,384]{3,2,1,0:T(8,128)(2,1)}, bf16[8,2,16,384]{3,2,1,0:T(8,128)(2,1)}, u32[]{:S(2)}, u32[]{:S(2)}) collective-permute-start(bf16[8,2,16,384]{3,2,1,0:T(8,128)(2,1)} %get-tuple-element.34), channel_id=1, source_target_pairs={{0,64},{32,96},{64,128},{96,160},{128,192},{160,224},{192,0},{224,... | collective-permute-start | bytes 589832 | tf_op jit(solution)/shard_map/ppermute | solution.py:256
  45.6 44.7 %copy-start.4 = (bf16[8,2,16,384]{3,2,1,0:T(8,128)(2,1)}, bf16[8,2,16,384]{3,2,1,0:T(8,128)(2,1)S(1)}, u32[]{:S(2)}) copy-start(bf16[8,2,16,384]{3,2,1,0:T(8,128)(2,1)S(1)} %collective-permute-done.7.rest_1_) | copy-start | bytes 589828
  48.2 47.1 %all-to-all-start.1 = ((bf16[32,2,16,640]{3,2,1,0:T(8,128)(2,1)}), bf16[32,2,16,640]{3,2,1,0:T(8,128)(2,1)}, u32[]{:S(2)}, u32[]{:S(2)}) async-start(bf16[32,2,16,640]{3,2,1,0:T(8,128)(2,1)} %select_pages.2), calls=%async_computation.1 | async-start | bytes 2621440 | tf_op jit(solution)/shard_map/all_to_all | solution.py:260
  59.1 14.1 %collective-permute-start.9 = (bf16[8,2,16,384]{3,2,1,0:T(8,128)(2,1)}, bf16[8,2,16,384]{3,2,1,0:T(8,128)(2,1)S(1)}, u32[]{:S(2)}, u32[]{:S(2)}) collective-permute-start(bf16[8,2,16,384]{3,2,1,0:T(8,128)(2,1)} %get-tuple-element.37), channel_id=1, source_target_pairs={{0,96},{32,64},{64,160},{96,128},{128,224},{160,192},{192,32},{224... | collective-permute-start | bytes 589832 | tf_op jit(solution)/shard_map/ppermute | solution.py:256
  62.2 16.0 %collective-permute-start.10 = (bf16[8,2,16,384]{3,2,1,0:T(8,128)(2,1)}, bf16[8,2,16,384]{3,2,1,0:T(8,128)(2,1)S(1)}, u32[]{:S(2)}, u32[]{:S(2)}) collective-permute-start(bf16[8,2,16,384]{3,2,1,0:T(8,128)(2,1)} %get-tuple-element.38), channel_id=1, source_target_pairs={{0,128},{32,160},{64,192},{96,224},{128,0},{160,32},{192,64},{224,... | collective-permute-start | bytes 589832 | tf_op jit(solution)/shard_map/ppermute | solution.py:256
  64.9 16.1 %collective-permute-start.11 = (bf16[8,2,16,384]{3,2,1,0:T(8,128)(2,1)}, bf16[8,2,16,384]{3,2,1,0:T(8,128)(2,1)S(1)}, u32[]{:S(2)}, u32[]{:S(2)}) collective-permute-start(bf16[8,2,16,384]{3,2,1,0:T(8,128)(2,1)} %get-tuple-element.39), channel_id=1, source_target_pairs={{0,160},{32,128},{64,224},{96,192},{128,32},{160,0},{192,96},{224,... | collective-permute-start | bytes 589832 | tf_op jit(solution)/shard_map/ppermute | solution.py:256
  64.9 16.1 %collective-permute-start.12 = (bf16[8,2,16,384]{3,2,1,0:T(8,128)(2,1)}, bf16[8,2,16,384]{3,2,1,0:T(8,128)(2,1)}, u32[]{:S(2)}, u32[]{:S(2)}) collective-permute-start(bf16[8,2,16,384]{3,2,1,0:T(8,128)(2,1)} %get-tuple-element.40), channel_id=1, source_target_pairs={{0,192},{32,224},{64,0},{96,32},{128,64},{160,96},{192,128},{224,1... | collective-permute-start | bytes 589832 | tf_op jit(solution)/shard_map/ppermute | solution.py:256
  68.4 22.0 %collective-permute-start.13 = (bf16[8,2,16,384]{3,2,1,0:T(8,128)(2,1)}, bf16[8,2,16,384]{3,2,1,0:T(8,128)(2,1)}, u32[]{:S(2)}, u32[]{:S(2)}) collective-permute-start(bf16[8,2,16,384]{3,2,1,0:T(8,128)(2,1)} %get-tuple-element.41), channel_id=1, source_target_pairs={{0,224},{32,192},{64,32},{96,0},{128,96},{160,64},{192,160},{224,1... | collective-permute-start | bytes 589832 | tf_op jit(solution)/shard_map/ppermute | solution.py:256
  73.2 17.1 %copy-start.5 = (bf16[8,2,16,384]{3,2,1,0:T(8,128)(2,1)}, bf16[8,2,16,384]{3,2,1,0:T(8,128)(2,1)S(1)}, u32[]{:S(2)}) copy-start(bf16[8,2,16,384]{3,2,1,0:T(8,128)(2,1)S(1)} %collective-permute-done.9.rest_3_) | copy-start | bytes 589828
  78.2 12.1 %copy-start.6 = (bf16[8,2,16,384]{3,2,1,0:T(8,128)(2,1)}, bf16[8,2,16,384]{3,2,1,0:T(8,128)(2,1)S(1)}, u32[]{:S(2)}) copy-start(bf16[8,2,16,384]{3,2,1,0:T(8,128)(2,1)S(1)} %collective-permute-done.10.rest_4_) | copy-start | bytes 589828
  81.1 9.3 %copy-start.7 = (bf16[8,2,16,384]{3,2,1,0:T(8,128)(2,1)}, bf16[8,2,16,384]{3,2,1,0:T(8,128)(2,1)S(1)}, u32[]{:S(2)}) copy-start(bf16[8,2,16,384]{3,2,1,0:T(8,128)(2,1)S(1)} %collective-permute-done.11.rest_5_) | copy-start | bytes 589828
  95.3 33.6 %all-to-all-start = ((bf16[32,2,16,384]{3,2,1,0:T(8,128)(2,1)}), bf16[32,2,16,384]{3,2,1,0:T(8,128)(2,1)S(1)}, u32[]{:S(2)}, u32[]{:S(2)}) async-start(bf16[32,2,16,384]{3,2,1,0:T(8,128)(2,1)} %select_pages.3), calls=%async_computation | async-start | bytes 1572864 | tf_op jit(solution)/shard_map/all_to_all | solution.py:260
  128.9 0.9 copy-start.1

commit v3 on v2

--- a/solution.py
+++ b/solution.py
@@ -21,7 +21,7 @@
 SHIFTS = [(dy, dx) for dy in range(RING) for dx in range(2)]
 CHUNKS = ((0, 5), (5, 3))
 ORDER = (1, 2, 3, 4, 5, 6, 7)
-TIE = 2
+TIE = 1
 DEPTH = 3
 MIB = 1024 * 1024
 
@@ -155,12 +155,12 @@
     return lax.broadcasted_iota(jnp.int32, (TILE, TILE), 0) >= lax.broadcasted_iota(jnp.int32, (TILE, TILE), 1)
 
 
-def prefix_pair(pulled_ref, valid):
-    prefix = pulled_ref.shape[0] * PAGE
+def prefix_pair(pulled_ref, pages, valid):
+    prefix = pages * PAGE
     ok = lax.broadcasted_iota(jnp.int32, (prefix, HEAD), 0) < valid
-    keys = pulled_ref[:, 0].reshape(prefix, HEAD).astype(jnp.float32)
+    keys = pulled_ref[:pages, 0].reshape(prefix, HEAD).astype(jnp.float32)
     keys = jnp.where(ok, keys, keys[0:1, :]).astype(jnp.bfloat16)
-    values = pulled_ref[:, 1].reshape(prefix, HEAD).astype(jnp.float32)
+    values = pulled_ref[:pages, 1].reshape(prefix, HEAD).astype(jnp.float32)
     values = jnp.where(ok, values, 0.0).astype(jnp.bfloat16)
     ones = jnp.where(ok, 1.0, 0.0).astype(jnp.bfloat16)
     return keys, jnp.concatenate([values, ones], axis=1)
@@ -171,9 +171,17 @@
 
 
 def attend_kernel(q_ref, pulled_ref, suffix_ref, count_ref, *rest):
-    o_ref = rest[-1]
     valid = count_ref[lax.axis_index("grp"), lax.axis_index("ep")] * PAGE
-    k_pre, v_pre = prefix_pair(pulled_ref, valid)
+    for pages in range(TILE // PAGE, pulled_ref.shape[0] + 1, TILE // PAGE):
+        end = pages * PAGE
+
+        @pl.when((valid > end - TILE) & (valid <= end))
+        def _(pages=pages):
+            attend_pages(pages, valid, q_ref, pulled_ref, suffix_ref, rest[-1])
+
+
+def attend_pages(pages, valid, q_ref, pulled_ref, suffix_ref, o_ref):
+    k_pre, v_pre = prefix_pair(pulled_ref, pages, valid)
     k_suf, v_suf = suffix_pair_of(suffix_ref)
     keys = jnp.concatenate([k_pre, k_suf], axis=0)
     values = jnp.concatenate([v_pre, v_suf], axis=0)
@@ -245,7 +253,7 @@
         in_specs=in_specs,
         out_specs=pl.BlockSpec((tokens, block), lambda h: (0, first + h)),
         input_output_aliases=aliases,
-        compiler_params=pltpu.CompilerParams(vmem_limit_bytes=63 * MIB),
+        compiler_params=pltpu.CompilerParams(vmem_limit_bytes=63 * MIB + 480 * 1024),
         cost_estimate=cost(heads, 768),
         name="attend",
     )(*operands)

time: 138 us -> 136 us (0.986)
  starting transfers between devices: 47.9 us -> 56.1 us
  waiting for transfers between devices: 53.9 us -> 46.5 us
  Pallas kernels: 34.1 us -> 30.9 us
    ppermute x14, waiting for transfers between devices: 40.9 us -> 32.5 us  [shift(): return lax.ppermute(page, 'grp', pairs)]
    ppermute x14, starting transfers between devices: 28.2 us -> 35 us  [shift(): return lax.ppermute(page, 'grp', pairs)]
    pallas_call x2, Pallas kernels: 22.2 us -> 19.1 us  [attend(): pl.pallas_call(attend_kernel, out_shape=jax.ShapeDtypeStruct((tokens, wid...]
    all_to_all x2, starting transfers between devices: 19.7 us -> 21.2 us  [exchange(): return lax.all_to_all(pages, 'ep', split_axis=0, concat_axis=0, tiled=True)]
  transfers between devices with their start and end apart: 16 -> 16, of which waited for: 11 -> 10; matrix products, arithmetic and copies ran while one was open for 0% -> 0% of each run, Pallas kernels for 15% -> 14%
where the time goes in v3:
time: 136 us; the launch traced here: 135 us
  starting transfers between devices  56.1 us (41%)
  waiting for transfers between devices  46.5 us (34%)
  Pallas kernels  30.9 us (23%)
  local copies, waits for them, and re-layouts  1.73 us (1%)
    ppermute x14, starting transfers between devices, shift(): return lax.ppermute(page, 'grp', pairs)  35 us
    ppermute x14, waiting for transfers between devices, shift(): return lax.ppermute(page, 'grp', pairs)  32.5 us
    all_to_all x2, starting transfers between devices, exchange(): return lax.all_to_all(pages, 'ep', split_axis=0, concat_axis=0, tiled=True)  21.2 us
    pallas_call x2, Pallas kernels, attend(): pl.pallas_call(attend_kernel, out_shape=jax.ShapeDtypeStruct((tokens, wid...  19.1 us
    all_to_all x2, waiting for transfers between devices, exchange(): return lax.all_to_all(pages, 'ep', split_axis=0, concat_axis=0, tiled=True)  14 us
    pallas_call x2, Pallas kernels, select(): pl.pallas_call(functools.partial(select_kernel, n_ep), out_shape=jax.Shap...  7.19 us
    pallas_call x1, Pallas kernels, pack(): pl.pallas_call(functools.partial(pack_kernel, holder.shape[1]), out_shape...  4.67 us
  transfers between devices with their start and end apart: 16, of which 10 were waited for; matrix products, arithmetic and copies ran while one was open for 0% of the time, Pallas kernels for 14%

profile of v3, /device:TPU:32, one launch (start us, length us, event | category | flops | bytes accessed | tf_op | source)
XLA Modules:
  0.0 135.4 jit_solution(10178544013147383055)
XLA Ops:
  0.0 0.0 copy-start
  0.0 0.9 copy-done
  0.9 0.1 constant_dynamic-slice_fusion
  1.0 0.7 copy.9
  1.7 4.7 %pack_pages.1 = (bf16[8,2,16,640]{3,2,1,0:T(8,128)(2,1)}, bf16[8,2,16,640]{3,2,1,0:T(8,128)(2,1)}, bf16[8,2,16,640]{3,2,1,0:T(8,128)(2,1)}, bf16[8,2,16,640]{3,2...) custom-call(s32[8,32]{1,0:T(8,128)} %holder_ref.5, ...), custom_call_target="tpu_custom_call" | custom-call | bytes 6291456 | tf_op jit(solution)/shard_map/pack_pages/pallas_call | solution.py:81
  6.4 1.5 %collective-permute-start = (bf16[8,2,16,640]{3,2,1,0:T(8,128)(2,1)}, bf16[8,2,16,640]{3,2,1,0:T(8,128)(2,1)S(1)}, u32[]{:S(2)}, u32[]{:S(2)}) collective-permute-start(bf16[8,2,16,640]{3,2,1,0:T(8,128)(2,1)} %get-tuple-element.25), channel_id=1, source_target_pairs={{0,32},{32,0},{64,96},{96,64},{128,160},{160,128},{192,224},{224,1... | collective-permute-start | bytes 983048 | tf_op jit(solution)/shard_map/ppermute | solution.py:264
  7.9 1.8 %collective-permute-start.1 = (bf16[8,2,16,640]{3,2,1,0:T(8,128)(2,1)}, bf16[8,2,16,640]{3,2,1,0:T(8,128)(2,1)S(1)}, u32[]{:S(2)}, u32[]{:S(2)}) collective-permute-start(bf16[8,2,16,640]{3,2,1,0:T(8,128)(2,1)} %get-tuple-element.26), channel_id=1, source_target_pairs={{0,64},{32,96},{64,128},{96,160},{128,192},{160,224},{192,0},{224,... | collective-permute-start | bytes 983048 | tf_op jit(solution)/shard_map/ppermute | solution.py:264
  9.7 1.7 %collective-permute-start.2 = (bf16[8,2,16,640]{3,2,1,0:T(8,128)(2,1)}, bf16[8,2,16,640]{3,2,1,0:T(8,128)(2,1)}, u32[]{:S(2)}, u32[]{:S(2)}) collective-permute-start(bf16[8,2,16,640]{3,2,1,0:T(8,128)(2,1)} %get-tuple-element.27), channel_id=1, source_target_pairs={{0,96},{32,64},{64,160},{96,128},{128,224},{160,192},{192,32},{224... | collective-permute-start | bytes 983048 | tf_op jit(solution)/shard_map/ppermute | solution.py:264
  11.4 1.2 collective-permute-start.3
  12.6 2.7 %collective-permute-start.4 = (bf16[8,2,16,640]{3,2,1,0:T(8,128)(2,1)}, bf16[8,2,16,640]{3,2,1,0:T(8,128)(2,1)}, u32[]{:S(2)}, u32[]{:S(2)}) collective-permute-start(bf16[8,2,16,640]{3,2,1,0:T(8,128)(2,1)} %get-tuple-element.29), channel_id=1, source_target_pairs={{0,160},{32,128},{64,224},{96,192},{128,32},{160,0},{192,96},{224,... | collective-permute-start | bytes 983048 | tf_op jit(solution)/shard_map/ppermute | solution.py:264
  15.4 1.9 %collective-permute-done.rest_1_ = bf16[8,2,16,640]{3,2,1,0:T(8,128)(2,1)S(1)} collective-permute-done((bf16[8,2,16,640]{3,2,1,0:T(8,128)(2,1)}, bf16[8,2,16,640]{3,2,1,0:T(8,128)(2,1)S(1)}, u32[]{:S(2)}, u32[]{:S(2)}) %collective-permute-start) | collective-permute-done | bytes 327712 | tf_op jit(solution)/shard_map/ppermute | solution.py:264
  17.3 3.0 %collective-permute-start.5 = (bf16[8,2,16,640]{3,2,1,0:T(8,128)(2,1)}, bf16[8,2,16,640]{3,2,1,0:T(8,128)(2,1)}, u32[]{:S(2)}, u32[]{:S(2)}) collective-permute-start(bf16[8,2,16,640]{3,2,1,0:T(8,128)(2,1)} %get-tuple-element.30), channel_id=1, source_target_pairs={{0,192},{32,224},{64,0},{96,32},{128,64},{160,96},{192,128},{224,1... | collective-permute-start | bytes 983048 | tf_op jit(solution)/shard_map/ppermute | solution.py:264
  20.3 12.0 %collective-permute-done.1.rest_2_ = bf16[8,2,16,640]{3,2,1,0:T(8,128)(2,1)S(1)} collective-permute-done((bf16[8,2,16,640]{3,2,1,0:T(8,128)(2,1)}, bf16[8,2,16,640]{3,2,1,0:T(8,128)(2,1)S(1)}, u32[]{:S(2)}, u32[]{:S(2)}) %collective-permute-start.1) | collective-permute-done | bytes 327712 | tf_op jit(solution)/shard_map/ppermute | solution.py:264
  32.3 3.5 %collective-permute-start.6 = (bf16[8,2,16,640]{3,2,1,0:T(8,128)(2,1)}, bf16[8,2,16,640]{3,2,1,0:T(8,128)(2,1)}, u32[]{:S(2)}, u32[]{:S(2)}) collective-permute-start(bf16[8,2,16,640]{3,2,1,0:T(8,128)(2,1)} %get-tuple-element.31), channel_id=1, source_target_pairs={{0,224},{32,192},{64,32},{96,0},{128,96},{160,64},{192,160},{224,1... | collective-permute-start | bytes 983048 | tf_op jit(solution)/shard_map/ppermute | solution.py:264
  35.9 0.0 collective-permute-done.2.rest_3_
  35.9 1.6 %collective-permute-start.7 = (bf16[8,2,16,384]{3,2,1,0:T(8,128)(2,1)}, bf16[8,2,16,384]{3,2,1,0:T(8,128)(2,1)S(1)}, u32[]{:S(2)}, u32[]{:S(2)}) collective-permute-start(bf16[8,2,16,384]{3,2,1,0:T(8,128)(2,1)} %get-tuple-element.32), channel_id=1, source_target_pairs={{0,32},{32,0},{64,96},{96,64},{128,160},{160,128},{192,224},{224,1... | collective-permute-start | bytes 589832 | tf_op jit(solution)/shard_map/ppermute | solution.py:264
  37.4 3.6 %collective-permute-done.3.rest_4_ = bf16[8,2,16,640]{3,2,1,0:T(8,128)(2,1)} collective-permute-done((bf16[8,2,16,640]{3,2,1,0:T(8,128)(2,1)}, bf16[8,2,16,640]{3,2,1,0:T(8,128)(2,1)}, u32[]{:S(2)}, u32[]{:S(2)}) %collective-permute-start.3) | collective-permute-done | bytes 327712 | tf_op jit(solution)/shard_map/ppermute | solution.py:264
  41.1 0.0 collective-permute-done.4.rest_5_
  41.1 0.6 collective-permute-done.5.rest_6_
  41.7 0.0 collective-permute-done.6.rest_7_
  41.7 0.0 copy-done.1
  41.7 0.0 copy-done.2
  41.7 3.8 %select_pages.2 = bf16[32,2,16,640]{3,2,1,0:T(8,128)(2,1)} custom-call(s32[8,32]{1,0:T(8,128)} %holder_ref.5, bf16[8,2,16,640]{3,2,1,0:T(8,128)(2,1)} %get-tuple-element.24.rest_0_, bf16[8,2,16,640]{3,2,1,0:T(8,128)(2,1)} %copy-done.1, bf16[8,2,16,640]{3,2,1,0:T(8,128)(2,1)} %copy-done.2, bf16[8,2,16,640]{3,2,1,0:T(8,128)(2,1)} %collective-permute-done.2.rest_3_, ...), custom_call_target="tpu_custom_call" | custom-call | bytes 6291456 | tf_op jit(solution)/shard_map/select_pages/pallas_call | solution.py:137
  45.5 0.0 collective-permute-done.7.rest_1_
  45.5 0.0 copy-start.3
  45.5 11.2 %all-to-all-start.1 = ((bf16[32,2,16,640]{3,2,1,0:T(8,128)(2,1)}), bf16[32,2,16,640]{3,2,1,0:T(8,128)(2,1)}, u32[]{:S(2)}, u32[]{:S(2)}) async-start(bf16[32,2,16,640]{3,2,1,0:T(8,128)(2,1)} %select_pages.2), calls=%async_computation.1 | async-start | bytes 2621440 | tf_op jit(solution)/shard_map/all_to_all | solution.py:268
  56.7 5.6 %collective-permute-start.8 = (bf16[8,2,16,384]{3,2,1,0:T(8,128)(2,1)}, bf16[8,2,16,384]{3,2,1,0:T(8,128)(2,1)S(1)}, u32[]{:S(2)}, u32[]{:S(2)}) collective-permute-start(bf16[8,2,16,384]{3,2,1,0:T(8,128)(2,1)} %get-tuple-element.34), channel_id=1, source_target_pairs={{0,64},{32,96},{64,128},{96,160},{128,192},{160,224},{192,0},{224,... | collective-permute-start | bytes 589832 | tf_op jit(solution)/shard_map/ppermute | solution.py:264
  62.4 2.3 %collective-permute-start.9 = (bf16[8,2,16,384]{3,2,1,0:T(8,128)(2,1)}, bf16[8,2,16,384]{3,2,1,0:T(8,128)(2,1)S(1)}, u32[]{:S(2)}, u32[]{:S(2)}) collective-permute-start(bf16[8,2,16,384]{3,2,1,0:T(8,128)(2,1)} %get-tuple-element.35), channel_id=1, source_target_pairs={{0,96},{32,64},{64,160},{96,128},{128,224},{160,192},{192,32},{224... | collective-permute-start | bytes 589832 | tf_op jit(solution)/shard_map/ppermute | solution.py:264
  64.7 0.0 collective-permute-start.10
  64.7 2.2 %collective-permute-start.11 = (bf16[8,2,16,384]{3,2,1,0:T(8,128)(2,1)}, bf16[8,2,16,384]{3,2,1,0:T(8,128)(2,1)}, u32[]{:S(2)}, u32[]{:S(2)}) collective-permute-start(bf16[8,2,16,384]{3,2,1,0:T(8,128)(2,1)} %get-tuple-element.37), channel_id=1, source_target_pairs={{0,160},{32,128},{64,224},{96,192},{128,32},{160,0},{192,96},{224,... | collective-permute-start | bytes 589832 | tf_op jit(solution)/shard_map/ppermute | solution.py:264
  66.9 3.1 %collective-permute-start.12 = (bf16[8,2,16,384]{3,2,1,0:T(8,128)(2,1)}, bf16[8,2,16,384]{3,2,1,0:T(8,128)(2,1)}, u32[]{:S(2)}, u32[]{:S(2)}) collective-permute-start(bf16[8,2,16,384]{3,2,1,0:T(8,128)(2,1)} %get-tuple-element.38), channel_id=1, source_target_pairs={{0,192},{32,224},{64,0},{96,32},{128,64},{160,96},{192,128},{224,1... | collective-permute-start | bytes 589832 | tf_op jit(solution)/shard_map/ppermute | solution.py:264
  70.0 2.0 %collective-permute-done.8.rest_2_ = bf16[8,2,16,384]{3,2,1,0:T(8,128)(2,1)S(1)} collective-permute-done((bf16[8,2,16,384]{3,2,1,0:T(8,128)(2,1)}, bf16[8,2,16,384]{3,2,1,0:T(8,128)(2,1)S(1)}, u32[]{:S(2)}, u32[]{:S(2)}) %collective-permute-start.8) | collective-permute-done | bytes 196640 | tf_op jit(solution)/shard_map/ppermute | solution.py:264
  72.1 4.6 %collective-permute-start.13 = (bf16[8,2,16,384]{3,2,1,0:T(8,128)(2,1)}, bf16[8,2,16,384]{3,2,1,0:T(8,128)(2,1)}, u32[]{:S(2)}, u32[]{:S(2)}) collective-permute-start(bf16[8,2,16,384]{3,2,1,0:T(8,128)(2,1)} %get-tuple-element.39), channel_id=1, source_target_pairs={{0,224},{32,192},{64,32},{96,0},{128,96},{160,64},{192,160},{224,1... | collective-permute-start | bytes 589832 | tf_op jit(solution)/shard_map/ppermute | solution.py:264
  76.6 0.0 collective-permute-done.9.rest_3_
  76.6 3.3 %collective-permute-done.10.rest_4_ = bf16[8,2,16,384]{3,2,1,0:T(8,128)(2,1)S(1)} collective-permute-done((bf16[8,2,16,384]{3,2,1,0:T(8,128)(2,1)}, bf16[8,2,16,384]{3,2,1,0:T(8,128)(2,1)S(1)}, u32[]{:S(2)}, u32[]{:S(2)}) %collective-permute-start.10) | collective-permute-done | bytes 196640 | tf_op jit(solution)/shard_map/ppermute | solution.py:264
  80.0 2.7 %collective-permute-done.11.rest_5_ = bf16[8,2,16,384]{3,2,1,0:T(8,128)(2,1)} collective-permute-done((bf16[8,2,16,384]{3,2,1,0:T(8,128)(2,1)}, bf16[8,2,16,384]{3,2,1,0:T(8,128)(2,1)}, u32[]{:S(2)}, u32[]{:S(2)}) %collective-permute-start.11) | collective-permute-done | bytes 196640 | tf_op jit(solution)/shard_map/ppermute | solution.py:264
  82.7 0.0 collective-permute-done.12.rest_6_
  82.7 6.3 %collective-permute-done.13.rest_7_ = bf16[8,2,16,384]{3,2,1,0:T(8,128)(2,1)} collective-permute-done((bf16[8,2,16,384]{3,2,1,0:T(8,128)(2,1)}, bf16[8,2,16,384]{3,2,1,0:T(8,128)(2,1)}, u32[]{:S(2)}, u32[]{:S(2)}) %collective-permute-start.13) | collective-permute-done | bytes 196640 | tf_op jit(solution)/shard_map/ppermute | solution.py:264
  89.0 0.0 copy-done.3
  89.0 0.0 copy-done.4
  89.0 0.0 copy-done.5
  89.0 0.0 copy-done.6
  89.0 3.4 %select_pages.3 = bf16[32,2,16,384]{3,2,1,0:T(8,128)(2,1)} custom-call(s32[8,32]{1,0:T(8,128)} %holder_ref.5, bf16[8,2,16,384]{3,2,1,0:T(8,128)(2,1)} %get-tuple-element.23.rest_0_, bf16[8,2,16,384]{3,2,1,0:T(8,128)(2,1)} %copy-done.3, bf16[8,2,16,384]{3,2,1,0:T(8,128)(2,1)} %copy-done.4, bf16[8,2,16,384]{3,2,1,0:T(8,128)(2,1)} %copy-done.5, ...), custom_call_target="tpu_custom_call" | custom-call | bytes 6291456 | tf_op jit(solution)/shard_map/select_pages/pallas_call | solution.py:137
  92.4 0.5 all-to-all-done.1.pulled_ref
  92.9 9.9 %all-to-all-start = ((bf16[32,2,16,384]{3,2,1,0:T(8,128)(2,1)}), bf16[32,2,16,384]{3,2,1,0:T(8,128)(2,1)}, u32[]{:S(2)}, u32[]{:S(2)}) async-start(bf16[32,2,16,384]{3,2,1,0:T(8,128)(2,1)} %select_pages.3), calls=%async_computation | async-start | bytes 1572864 | tf_op jit(solution)/shard_map/all_to_all | solution.py:268
  102.8 11.4 %attend.2.rest_0_ = bf16[384,5120]{1,0:T(8,128)(2,1)} custom-call(bf16[384,5120]{1,0:T(8,128)(2,1)} %bitcast.5, bf16[32,2,16,640]{3,2,1,0:T(8,128)(2,1)} %all-to-all-done.1.pulled_ref, bf16[2,384,1024]{2,1,0:T(8,128)(2,1)} %bitcast.7, s32[8,32]{1,0:T(8,128)} %count_ref.3), custom_call_target="tpu_custom_call" | custom-call | flops 3774873600 | bytes 7864320 | tf_op jit(solution)/shard_map/attend/pallas_call | solution.py:249
  114.3 13.5 %all-to-all-done.pulled_ref = bf16[32,2,16,384]{3,2,1,0:T(8,128)(2,1)} async-done(((bf16[32,2,16,384]{3,2,1,0:T(8,128)(2,1)}), bf16[32,2,16,384]{3,2,1,0:T(8,128)(2,1)}, u32[]{:S(2)}, u32[]{:S(2)}) %all-to-all-start) | async-done | bytes 786464 | tf_op jit(solution)/shard_map/all_to_all | solution.py:268
  127.8 7.6 %attend.3 = bf16[384,5120]{1,0:T(8,128)(2,1)} custom-call(bf16[384,5120]{1,0:T(8,128)(2,1)} %bitcast.6, bf16[32,2,16,384]{3,2,1,0:T(8,128)(2,1)} %all-to-all-done.pulled_ref, bf16[2,384,1024]{2,1,0:T(8,128)(2,1)} %bitcast.8, s32[8,32]{1,0:T(8,128)} %count_ref.3, bf16[384,5120]{1,0:T(8,128)(2,1)} %attend.2.rest_0_), custom_call_target="tpu_custom_call", output_to_operand_aliasing={{}: (4, {})} | custom-call | flops 2264924160 | bytes 4718592 | tf_op jit(solution)/shard_map/attend/pallas_call | solution.py:249
  (5 shorter events, 0.0 us)
Async XLA Ops:
  0.0 0.9 copy-start
  6.4 10.9 %collective-permute-start = (bf16[8,2,16,640]{3,2,1,0:T(8,128)(2,1)}, bf16[8,2,16,640]{3,2,1,0:T(8,128)(2,1)S(1)}, u32[]{:S(2)}, u32[]{:S(2)}) collective-permute-start(bf16[8,2,16,640]{3,2,1,0:T(8,128)(2,1)} %get-tuple-element.25), channel_id=1, source_target_pairs={{0,32},{32,0},{64,96},{96,64},{128,160},{160,128},{192,224},{224,1... | collective-permute-start | bytes 983048 | tf_op jit(solution)/shard_map/ppermute | solution.py:264
  7.9 24.4 %collective-permute-start.1 = (bf16[8,2,16,640]{3,2,1,0:T(8,128)(2,1)}, bf16[8,2,16,640]{3,2,1,0:T(8,128)(2,1)S(1)}, u32[]{:S(2)}, u32[]{:S(2)}) collective-permute-start(bf16[8,2,16,640]{3,2,1,0:T(8,128)(2,1)} %get-tuple-element.26), channel_id=1, source_target_pairs={{0,64},{32,96},{64,128},{96,160},{128,192},{160,224},{192,0},{224,... | collective-permute-start | bytes 983048 | tf_op jit(solution)/shard_map/ppermute | solution.py:264
  9.7 26.2 %collective-permute-start.2 = (bf16[8,2,16,640]{3,2,1,0:T(8,128)(2,1)}, bf16[8,2,16,640]{3,2,1,0:T(8,128)(2,1)}, u32[]{:S(2)}, u32[]{:S(2)}) collective-permute-start(bf16[8,2,16,640]{3,2,1,0:T(8,128)(2,1)} %get-tuple-element.27), channel_id=1, source_target_pairs={{0,96},{32,64},{64,160},{96,128},{128,224},{160,192},{192,32},{224... | collective-permute-start | bytes 983048 | tf_op jit(solution)/shard_map/ppermute | solution.py:264
  11.4 29.6 %collective-permute-start.3 = (bf16[8,2,16,640]{3,2,1,0:T(8,128)(2,1)}, bf16[8,2,16,640]{3,2,1,0:T(8,128)(2,1)}, u32[]{:S(2)}, u32[]{:S(2)}) collective-permute-start(bf16[8,2,16,640]{3,2,1,0:T(8,128)(2,1)} %get-tuple-element.28), channel_id=1, source_target_pairs={{0,128},{32,160},{64,192},{96,224},{128,0},{160,32},{192,64},{224,... | collective-permute-start | bytes 983048 | tf_op jit(solution)/shard_map/ppermute | solution.py:264
  12.6 28.4 %collective-permute-start.4 = (bf16[8,2,16,640]{3,2,1,0:T(8,128)(2,1)}, bf16[8,2,16,640]{3,2,1,0:T(8,128)(2,1)}, u32[]{:S(2)}, u32[]{:S(2)}) collective-permute-start(bf16[8,2,16,640]{3,2,1,0:T(8,128)(2,1)} %get-tuple-element.29), channel_id=1, source_target_pairs={{0,160},{32,128},{64,224},{96,192},{128,32},{160,0},{192,96},{224,... | collective-permute-start | bytes 983048 | tf_op jit(solution)/shard_map/ppermute | solution.py:264
  17.3 24.4 %copy-start.1 = (bf16[8,2,16,640]{3,2,1,0:T(8,128)(2,1)}, bf16[8,2,16,640]{3,2,1,0:T(8,128)(2,1)S(1)}, u32[]{:S(2)}) copy-start(bf16[8,2,16,640]{3,2,1,0:T(8,128)(2,1)S(1)} %collective-permute-done.rest_1_) | copy-start | bytes 983044
  17.3 24.4 %collective-permute-start.5 = (bf16[8,2,16,640]{3,2,1,0:T(8,128)(2,1)}, bf16[8,2,16,640]{3,2,1,0:T(8,128)(2,1)}, u32[]{:S(2)}, u32[]{:S(2)}) collective-permute-start(bf16[8,2,16,640]{3,2,1,0:T(8,128)(2,1)} %get-tuple-element.30), channel_id=1, source_target_pairs={{0,192},{32,224},{64,0},{96,32},{128,64},{160,96},{192,128},{224,1... | collective-permute-start | bytes 983048 | tf_op jit(solution)/shard_map/ppermute | solution.py:264
  32.3 9.4 %copy-start.2 = (bf16[8,2,16,640]{3,2,1,0:T(8,128)(2,1)}, bf16[8,2,16,640]{3,2,1,0:T(8,128)(2,1)S(1)}, u32[]{:S(2)}) copy-start(bf16[8,2,16,640]{3,2,1,0:T(8,128)(2,1)S(1)} %collective-permute-done.1.rest_2_) | copy-start | bytes 983044
  32.3 9.4 %collective-permute-start.6 = (bf16[8,2,16,640]{3,2,1,0:T(8,128)(2,1)}, bf16[8,2,16,640]{3,2,1,0:T(8,128)(2,1)}, u32[]{:S(2)}, u32[]{:S(2)}) collective-permute-start(bf16[8,2,16,640]{3,2,1,0:T(8,128)(2,1)} %get-tuple-element.31), channel_id=1, source_target_pairs={{0,224},{32,192},{64,32},{96,0},{128,96},{160,64},{192,160},{224,1... | collective-permute-start | bytes 983048 | tf_op jit(solution)/shard_map/ppermute | solution.py:264
  35.9 9.6 %collective-permute-start.7 = (bf16[8,2,16,384]{3,2,1,0:T(8,128)(2,1)}, bf16[8,2,16,384]{3,2,1,0:T(8,128)(2,1)S(1)}, u32[]{:S(2)}, u32[]{:S(2)}) collective-permute-start(bf16[8,2,16,384]{3,2,1,0:T(8,128)(2,1)} %get-tuple-element.32), channel_id=1, source_target_pairs={{0,32},{32,0},{64,96},{96,64},{128,160},{160,128},{192,224},{224,1... | collective-permute-start | bytes 589832 | tf_op jit(solution)/shard_map/ppermute | solution.py:264
  45.5 43.5 %copy-start.3 = (bf16[8,2,16,384]{3,2,1,0:T(8,128)(2,1)}, bf16[8,2,16,384]{3,2,1,0:T(8,128)(2,1)S(1)}, u32[]{:S(2)}) copy-start(bf16[8,2,16,384]{3,2,1,0:T(8,128)(2,1)S(1)} %collective-permute-done.7.rest_1_) | copy-start | bytes 589828
  45.5 47.4 %all-to-all-start.1 = ((bf16[32,2,16,640]{3,2,1,0:T(8,128)(2,1)}), bf16[32,2,16,640]{3,2,1,0:T(8,128)(2,1)}, u32[]{:S(2)}, u32[]{:S(2)}) async-start(bf16[32,2,16,640]{3,2,1,0:T(8,128)(2,1)} %select_pages.2), calls=%async_computation.1 | async-start | bytes 2621440 | tf_op jit(solution)/shard_map/all_to_all | solution.py:268
  56.7 15.3 %collective-permute-start.8 = (bf16[8,2,16,384]{3,2,1,0:T(8,128)(2,1)}, bf16[8,2,16,384]{3,2,1,0:T(8,128)(2,1)S(1)}, u32[]{:S(2)}, u32[]{:S(2)}) collective-permute-start(bf16[8,2,16,384]{3,2,1,0:T(8,128)(2,1)} %get-tuple-element.34), channel_id=1, source_target_pairs={{0,64},{32,96},{64,128},{96,160},{128,192},{160,224},{192,0},{224,... | collective-permute-start | bytes 589832 | tf_op jit(solution)/shard_map/ppermute | solution.py:264
  62.4 14.3 %collective-permute-start.9 = (bf16[8,2,16,384]{3,2,1,0:T(8,128)(2,1)}, bf16[8,2,16,384]{3,2,1,0:T(8,128)(2,1)S(1)}, u32[]{:S(2)}, u32[]{:S(2)}) collective-permute-start(bf16[8,2,16,384]{3,2,1,0:T(8,128)(2,1)} %get-tuple-element.35), channel_id=1, source_target_pairs={{0,96},{32,64},{64,160},{96,128},{128,224},{160,192},{192,32},{224... | collective-permute-start | bytes 589832 | tf_op jit(solution)/shard_map/ppermute | solution.py:264
  64.7 15.3 %collective-permute-start.10 = (bf16[8,2,16,384]{3,2,1,0:T(8,128)(2,1)}, bf16[8,2,16,384]{3,2,1,0:T(8,128)(2,1)S(1)}, u32[]{:S(2)}, u32[]{:S(2)}) collective-permute-start(bf16[8,2,16,384]{3,2,1,0:T(8,128)(2,1)} %get-tuple-element.36), channel_id=1, source_target_pairs={{0,128},{32,160},{64,192},{96,224},{128,0},{160,32},{192,64},{224,... | collective-permute-start | bytes 589832 | tf_op jit(solution)/shard_map/ppermute | solution.py:264
  64.7 18.0 %collective-permute-start.11 = (bf16[8,2,16,384]{3,2,1,0:T(8,128)(2,1)}, bf16[8,2,16,384]{3,2,1,0:T(8,128)(2,1)}, u32[]{:S(2)}, u32[]{:S(2)}) collective-permute-start(bf16[8,2,16,384]{3,2,1,0:T(8,128)(2,1)} %get-tuple-element.37), channel_id=1, source_target_pairs={{0,160},{32,128},{64,224},{96,192},{128,32},{160,0},{192,96},{224,... | collective-permute-start | bytes 589832 | tf_op jit(solution)/shard_map/ppermute | solution.py:264
  66.9 15.8 %collective-permute-start.12 = (bf16[8,2,16,384]{3,2,1,0:T(8,128)(2,1)}, bf16[8,2,16,384]{3,2,1,0:T(8,128)(2,1)}, u32[]{:S(2)}, u32[]{:S(2)}) collective-permute-start(bf16[8,2,16,384]{3,2,1,0:T(8,128)(2,1)} %get-tuple-element.38), channel_id=1, source_target_pairs={{0,192},{32,224},{64,0},{96,32},{128,64},{160,96},{192,128},{224,1... | collective-permute-start | bytes 589832 | tf_op jit(solution)/shard_map/ppermute | solution.py:264
  72.1 16.9 %copy-start.4 = (bf16[8,2,16,384]{3,2,1,0:T(8,128)(2,1)}, bf16[8,2,16,384]{3,2,1,0:T(8,128)(2,1)S(1)}, u32[]{:S(2)}) copy-start(bf16[8,2,16,384]{3,2,1,0:T(8,128)(2,1)S(1)} %collective-permute-done.8.rest_2_) | copy-start | bytes 589828
  72.1 16.9 %collective-permute-start.13 = (bf16[8,2,16,384]{3,2,1,0:T(8,128)(2,1)}, bf16[8,2,16,384]{3,2,1,0:T(8,128)(2,1)}, u32[]{:S(2)}, u32[]{:S(2)}) collective-permute-start(bf16[8,2,16,384]{3,2,1,0:T(8,128)(2,1)} %get-tuple-element.39), channel_id=1, source_target_pairs={{0,224},{32,192},{64,32},{96,0},{128,96},{160,64},{192,160},{224,1... | collective-permute-start | bytes 589832 | tf_op jit(solution)/shard_map/ppermute | solution.py:264
  76.6 12.4 %copy-start.5 = (bf16[8,2,16,384]{3,2,1,0:T(8,128)(2,1)}, bf16[8,2,16,384]{3,2,1,0:T(8,128)(2,1)S(1)}, u32[]{:S(2)}) copy-start(bf16[8,2,16,384]{3,2,1,0:T(8,128)(2,1)S(1)} %collective-permute-done.9.rest_3_) | copy-start | bytes 589828
  80.0 9.0 %copy-start.6 = (bf16[8,2,16,384]{3,2,1,0:T(8,128)(2,1)}, bf16[8,2,16,384]{3,2,1,0:T(8,128)(2,1)S(1)}, u32[]{:S(2)}) copy-start(bf16[8,2,16,384]{3,2,1,0:T(8,128)(2,1)S(1)} %collective-permute-done.10.rest_4_) | copy-start | bytes 589828
  92.9 34.9 %all-to-all-start = ((bf16[32,2,16,384]{3,2,1,0:T(8,128)(2,1)}), bf16[32,2,16,384]{3,2,1,0:T(8,128)(2,1)}, u32[]{:S(2)}, u32[]{:S(2)}) async-start(bf16[32,2,16,384]{3,2,1,0:T(8,128)(2,1)} %select_pages.3), calls=%async_computation | async-start | bytes 1572864 | tf_op jit(solution)/shard_map/all_to_all | solution.py:268

commit v4 on v3

--- a/solution.py
+++ b/solution.py
@@ -22,6 +22,7 @@
 CHUNKS = ((0, 5), (5, 3))
 ORDER = (1, 2, 3, 4, 5, 6, 7)
 TIE = 1
+ORDERS = ((0, 2, 6, 1, 5, 3, 7, 4), (0, 1, 2, 3, 4, 5, 6, 7))
 DEPTH = 3
 MIB = 1024 * 1024
 
@@ -102,10 +103,10 @@
     return [outs[c * n : (c + 1) * n] for c in range(len(CHUNKS))]
 
 
-def select_kernel(n_ep, holder_ref, *rest):
+def select_kernel(order, n_ep, holder_ref, *rest):
     arrived, (out_ref, count_ref, held, sem, out_sem) = rest[: len(SHIFTS)], rest[len(SHIFTS) :]
     me = lax.axis_index("grp")
-    loads = [pltpu.make_async_copy(arrived[s], held.at[s], sem.at[s]) for s in range(len(SHIFTS))]
+    loads = [pltpu.make_async_copy(pages, held.at[s], sem.at[s]) for pages, s in zip(arrived, order)]
     for load in loads:
         load.start()
     for s in range(len(SHIFTS)):
@@ -130,12 +131,12 @@
     lax.fori_loop(0, n_ep, drain, 0, unroll=8)
 
 
-def select(holder, arrived):
+def select(order, holder, arrived):
     n_ep = holder.shape[1]
     one = arrived[0].shape[1:]
     dtype = arrived[0].dtype
     return pl.pallas_call(
-        functools.partial(select_kernel, n_ep),
+        functools.partial(select_kernel, order, n_ep),
         out_shape=jax.ShapeDtypeStruct((n_ep,) + one, dtype),
         in_specs=[pl.BlockSpec(memory_space=SMEM)] + [pl.BlockSpec(memory_space=pl.ANY)] * len(SHIFTS),
         out_specs=pl.BlockSpec(memory_space=pl.ANY),
@@ -148,7 +149,7 @@
         compiler_params=pltpu.CompilerParams(vmem_limit_bytes=63 * MIB),
         cost_estimate=pl.CostEstimate(flops=0, bytes_accessed=6 * MIB, transcendentals=0),
         name="select_pages",
-    )(holder, *arrived)
+    )(holder, *[arrived[s] for s in order])
 
 
 def triangle():
@@ -280,7 +281,7 @@
         arrived.append([got[s] for s in range(len(SHIFTS))])
     pulled = []
     for c in range(len(CHUNKS)):
-        forward = select(holder, arrived[c])
+        forward = select(ORDERS[c], holder, arrived[c])
         if TIE and c + 1 < len(CHUNKS):
             tied = [arrived[c + 1][s] for s in ORDER[:TIE]]
             forward, tied = lax.optimization_barrier((forward, tied))

time: 136 us -> 135 us (level)
  starting transfers between devices: 56.1 us -> 40.9 us
  waiting for transfers between devices: 46.5 us -> 59.6 us
    ppermute x14, starting transfers between devices: 35 us -> 22.9 us  [shift(): return lax.ppermute(page, 'grp', pairs)]
    ppermute x14, waiting for transfers between devices: 32.5 us -> 41.7 us  [shift(): return lax.ppermute(page, 'grp', pairs)]
    all_to_all x2, waiting for transfers between devices: 14 us -> 17.9 us  [exchange(): return lax.all_to_all(pages, 'ep', split_axis=0, concat_axis=0, tiled=True)]
    all_to_all x2, starting transfers between devices: 21.2 us -> 18 us  [exchange(): return lax.all_to_all(pages, 'ep', split_axis=0, concat_axis=0, tiled=True)]
where the time goes in v4:
time: 135 us; the launch traced here: 134 us
  waiting for transfers between devices  59.6 us (44%)
  starting transfers between devices  40.9 us (30%)
  Pallas kernels  31.2 us (23%)
  local copies, waits for them, and re-layouts  1.73 us (1%)
    ppermute x14, waiting for transfers between devices, shift(): return lax.ppermute(page, 'grp', pairs)  41.7 us
    ppermute x14, starting transfers between devices, shift(): return lax.ppermute(page, 'grp', pairs)  22.9 us
    pallas_call x2, Pallas kernels, attend(): pl.pallas_call(attend_kernel, out_shape=jax.ShapeDtypeStruct((tokens, wid...  19.1 us
    all_to_all x2, starting transfers between devices, exchange(): return lax.all_to_all(pages, 'ep', split_axis=0, concat_axis=0, tiled=True)  18 us
    all_to_all x2, waiting for transfers between devices, exchange(): return lax.all_to_all(pages, 'ep', split_axis=0, concat_axis=0, tiled=True)  17.9 us
    pallas_call x2, Pallas kernels, select(): pl.pallas_call(functools.partial(select_kernel, order, n_ep), out_shape=j...  7.19 us
    pallas_call x1, Pallas kernels, pack(): pl.pallas_call(functools.partial(pack_kernel, holder.shape[1]), out_shape...  4.94 us
  transfers between devices with their start and end apart: 16, of which 10 were waited for; matrix products, arithmetic and copies ran while one was open for 0% of the time, Pallas kernels for 14%

profile of v4, /device:TPU:32, one launch (start us, length us, event | category | flops | bytes accessed | tf_op | source)
XLA Modules:
  0.0 133.5 jit_solution(1885188935545950033)
XLA Ops:
  0.0 0.0 copy-start
  0.0 0.9 copy-done
  0.9 0.1 constant_dynamic-slice_fusion
  1.0 0.7 copy.9
  1.7 4.9 %pack_pages.1 = (bf16[8,2,16,640]{3,2,1,0:T(8,128)(2,1)}, bf16[8,2,16,640]{3,2,1,0:T(8,128)(2,1)}, bf16[8,2,16,640]{3,2,1,0:T(8,128)(2,1)}, bf16[8,2,16,640]{3,2...) custom-call(s32[8,32]{1,0:T(8,128)} %holder_ref.5, ...), custom_call_target="tpu_custom_call" | custom-call | bytes 6291456 | tf_op jit(solution)/shard_map/pack_pages/pallas_call | solution.py:82
  6.7 1.6 %collective-permute-start = (bf16[8,2,16,640]{3,2,1,0:T(8,128)(2,1)}, bf16[8,2,16,640]{3,2,1,0:T(8,128)(2,1)S(1)}, u32[]{:S(2)}, u32[]{:S(2)}) collective-permute-start(bf16[8,2,16,640]{3,2,1,0:T(8,128)(2,1)} %get-tuple-element.25), channel_id=1, source_target_pairs={{0,64},{32,96},{64,128},{96,160},{128,192},{160,224},{192,0},{224,... | collective-permute-start | bytes 983048 | tf_op jit(solution)/shard_map/ppermute | solution.py:265
  8.3 1.7 %collective-permute-start.1 = (bf16[8,2,16,640]{3,2,1,0:T(8,128)(2,1)}, bf16[8,2,16,640]{3,2,1,0:T(8,128)(2,1)S(1)}, u32[]{:S(2)}, u32[]{:S(2)}) collective-permute-start(bf16[8,2,16,640]{3,2,1,0:T(8,128)(2,1)} %get-tuple-element.26), channel_id=1, source_target_pairs={{0,192},{32,224},{64,0},{96,32},{128,64},{160,96},{192,128},{224,1... | collective-permute-start | bytes 983048 | tf_op jit(solution)/shard_map/ppermute | solution.py:265
  10.0 1.4 %collective-permute-start.2 = (bf16[8,2,16,640]{3,2,1,0:T(8,128)(2,1)}, bf16[8,2,16,640]{3,2,1,0:T(8,128)(2,1)}, u32[]{:S(2)}, u32[]{:S(2)}) collective-permute-start(bf16[8,2,16,640]{3,2,1,0:T(8,128)(2,1)} %get-tuple-element.27), channel_id=1, source_target_pairs={{0,32},{32,0},{64,96},{96,64},{128,160},{160,128},{192,224},{224,1... | collective-permute-start | bytes 983048 | tf_op jit(solution)/shard_map/ppermute | solution.py:265
  11.4 1.8 %collective-permute-start.3 = (bf16[8,2,16,640]{3,2,1,0:T(8,128)(2,1)}, bf16[8,2,16,640]{3,2,1,0:T(8,128)(2,1)}, u32[]{:S(2)}, u32[]{:S(2)}) collective-permute-start(bf16[8,2,16,640]{3,2,1,0:T(8,128)(2,1)} %get-tuple-element.28), channel_id=1, source_target_pairs={{0,160},{32,128},{64,224},{96,192},{128,32},{160,0},{192,96},{224,... | collective-permute-start | bytes 983048 | tf_op jit(solution)/shard_map/ppermute | solution.py:265
  13.2 1.8 %collective-permute-start.4 = (bf16[8,2,16,640]{3,2,1,0:T(8,128)(2,1)}, bf16[8,2,16,640]{3,2,1,0:T(8,128)(2,1)}, u32[]{:S(2)}, u32[]{:S(2)}) collective-permute-start(bf16[8,2,16,640]{3,2,1,0:T(8,128)(2,1)} %get-tuple-element.29), channel_id=1, source_target_pairs={{0,96},{32,64},{64,160},{96,128},{128,224},{160,192},{192,32},{224... | collective-permute-start | bytes 983048 | tf_op jit(solution)/shard_map/ppermute | solution.py:265
  15.0 2.6 %collective-permute-done.rest_1_ = bf16[8,2,16,640]{3,2,1,0:T(8,128)(2,1)S(1)} collective-permute-done((bf16[8,2,16,640]{3,2,1,0:T(8,128)(2,1)}, bf16[8,2,16,640]{3,2,1,0:T(8,128)(2,1)S(1)}, u32[]{:S(2)}, u32[]{:S(2)}) %collective-permute-start) | collective-permute-done | bytes 327712 | tf_op jit(solution)/shard_map/ppermute | solution.py:265
  17.6 3.1 %collective-permute-start.5 = (bf16[8,2,16,640]{3,2,1,0:T(8,128)(2,1)}, bf16[8,2,16,640]{3,2,1,0:T(8,128)(2,1)}, u32[]{:S(2)}, u32[]{:S(2)}) collective-permute-start(bf16[8,2,16,640]{3,2,1,0:T(8,128)(2,1)} %get-tuple-element.30), channel_id=1, source_target_pairs={{0,224},{32,192},{64,32},{96,0},{128,96},{160,64},{192,160},{224,1... | collective-permute-start | bytes 983048 | tf_op jit(solution)/shard_map/ppermute | solution.py:265
  20.7 0.0 collective-permute-done.1.rest_2_
  20.7 0.2 collective-permute-start.6
  20.9 0.0 collective-permute-done.2.rest_3_
  20.9 1.7 %collective-permute-start.7 = (bf16[8,2,16,384]{3,2,1,0:T(8,128)(2,1)}, bf16[8,2,16,384]{3,2,1,0:T(8,128)(2,1)S(1)}, u32[]{:S(2)}, u32[]{:S(2)}) collective-permute-start(bf16[8,2,16,384]{3,2,1,0:T(8,128)(2,1)} %get-tuple-element.32), channel_id=1, source_target_pairs={{0,32},{32,0},{64,96},{96,64},{128,160},{160,128},{192,224},{224,1... | collective-permute-start | bytes 589832 | tf_op jit(solution)/shard_map/ppermute | solution.py:265
  22.6 6.9 %collective-permute-done.3.rest_4_ = bf16[8,2,16,640]{3,2,1,0:T(8,128)(2,1)} collective-permute-done((bf16[8,2,16,640]{3,2,1,0:T(8,128)(2,1)}, bf16[8,2,16,640]{3,2,1,0:T(8,128)(2,1)}, u32[]{:S(2)}, u32[]{:S(2)}) %collective-permute-start.3) | collective-permute-done | bytes 327712 | tf_op jit(solution)/shard_map/ppermute | solution.py:265
  29.6 6.7 %collective-permute-done.4.rest_5_ = bf16[8,2,16,640]{3,2,1,0:T(8,128)(2,1)} collective-permute-done((bf16[8,2,16,640]{3,2,1,0:T(8,128)(2,1)}, bf16[8,2,16,640]{3,2,1,0:T(8,128)(2,1)}, u32[]{:S(2)}, u32[]{:S(2)}) %collective-permute-start.4) | collective-permute-done | bytes 327712 | tf_op jit(solution)/shard_map/ppermute | solution.py:265
  36.3 6.7 %collective-permute-done.5.rest_6_ = bf16[8,2,16,640]{3,2,1,0:T(8,128)(2,1)} collective-permute-done((bf16[8,2,16,640]{3,2,1,0:T(8,128)(2,1)}, bf16[8,2,16,640]{3,2,1,0:T(8,128)(2,1)}, u32[]{:S(2)}, u32[]{:S(2)}) %collective-permute-start.5) | collective-permute-done | bytes 327712 | tf_op jit(solution)/shard_map/ppermute | solution.py:265
  43.0 0.0 collective-permute-done.6.rest_7_
  43.0 0.0 copy-done.1
  43.0 0.0 copy-done.2
  43.0 3.8 %select_pages.2 = bf16[32,2,16,640]{3,2,1,0:T(8,128)(2,1)} custom-call(s32[8,32]{1,0:T(8,128)} %holder_ref.5, bf16[8,2,16,640]{3,2,1,0:T(8,128)(2,1)} %get-tuple-element.24.rest_0_, bf16[8,2,16,640]{3,2,1,0:T(8,128)(2,1)} %copy-done.1, bf16[8,2,16,640]{3,2,1,0:T(8,128)(2,1)} %copy-done.2, bf16[8,2,16,640]{3,2,1,0:T(8,128)(2,1)} %collective-permute-done.2.rest_3_, ...), custom_call_target="tpu_custom_call" | custom-call | bytes 6291456 | tf_op jit(solution)/shard_map/select_pages/pallas_call | solution.py:138
  46.8 0.0 collective-permute-done.7.rest_1_
  46.8 0.0 copy-start.3
  46.8 11.2 %all-to-all-start.1 = ((bf16[32,2,16,640]{3,2,1,0:T(8,128)(2,1)}), bf16[32,2,16,640]{3,2,1,0:T(8,128)(2,1)}, u32[]{:S(2)}, u32[]{:S(2)}) async-start(bf16[32,2,16,640]{3,2,1,0:T(8,128)(2,1)} %select_pages.2), calls=%async_computation.1 | async-start | bytes 2621440 | tf_op jit(solution)/shard_map/all_to_all | solution.py:269
  58.0 0.9 collective-permute-start.8
  58.9 0.9 collective-permute-start.9
  59.9 3.1 %collective-permute-start.10 = (bf16[8,2,16,384]{3,2,1,0:T(8,128)(2,1)}, bf16[8,2,16,384]{3,2,1,0:T(8,128)(2,1)S(1)}, u32[]{:S(2)}, u32[]{:S(2)}) collective-permute-start(bf16[8,2,16,384]{3,2,1,0:T(8,128)(2,1)} %get-tuple-element.36), channel_id=1, source_target_pairs={{0,128},{32,160},{64,192},{96,224},{128,0},{160,32},{192,64},{224,... | collective-permute-start | bytes 589832 | tf_op jit(solution)/shard_map/ppermute | solution.py:265
  63.0 1.3 collective-permute-start.11
  64.3 2.3 %collective-permute-start.12 = (bf16[8,2,16,384]{3,2,1,0:T(8,128)(2,1)}, bf16[8,2,16,384]{3,2,1,0:T(8,128)(2,1)}, u32[]{:S(2)}, u32[]{:S(2)}) collective-permute-start(bf16[8,2,16,384]{3,2,1,0:T(8,128)(2,1)} %get-tuple-element.38), channel_id=1, source_target_pairs={{0,192},{32,224},{64,0},{96,32},{128,64},{160,96},{192,128},{224,1... | collective-permute-start | bytes 589832 | tf_op jit(solution)/shard_map/ppermute | solution.py:265
  66.6 5.3 %collective-permute-done.8.rest_2_ = bf16[8,2,16,384]{3,2,1,0:T(8,128)(2,1)S(1)} collective-permute-done((bf16[8,2,16,384]{3,2,1,0:T(8,128)(2,1)}, bf16[8,2,16,384]{3,2,1,0:T(8,128)(2,1)S(1)}, u32[]{:S(2)}, u32[]{:S(2)}) %collective-permute-start.8) | collective-permute-done | bytes 196640 | tf_op jit(solution)/shard_map/ppermute | solution.py:265
  71.9 1.0 collective-permute-start.13
  72.9 0.0 collective-permute-done.9.rest_3_
  72.9 6.0 %collective-permute-done.10.rest_4_ = bf16[8,2,16,384]{3,2,1,0:T(8,128)(2,1)S(1)} collective-permute-done((bf16[8,2,16,384]{3,2,1,0:T(8,128)(2,1)}, bf16[8,2,16,384]{3,2,1,0:T(8,128)(2,1)S(1)}, u32[]{:S(2)}, u32[]{:S(2)}) %collective-permute-start.10) | collective-permute-done | bytes 196640 | tf_op jit(solution)/shard_map/ppermute | solution.py:265
  78.8 1.6 %collective-permute-done.11.rest_5_ = bf16[8,2,16,384]{3,2,1,0:T(8,128)(2,1)} collective-permute-done((bf16[8,2,16,384]{3,2,1,0:T(8,128)(2,1)}, bf16[8,2,16,384]{3,2,1,0:T(8,128)(2,1)}, u32[]{:S(2)}, u32[]{:S(2)}) %collective-permute-start.11) | collective-permute-done | bytes 196640 | tf_op jit(solution)/shard_map/ppermute | solution.py:265
  80.4 0.0 collective-permute-done.12.rest_6_
  80.4 5.9 %collective-permute-done.13.rest_7_ = bf16[8,2,16,384]{3,2,1,0:T(8,128)(2,1)} collective-permute-done((bf16[8,2,16,384]{3,2,1,0:T(8,128)(2,1)}, bf16[8,2,16,384]{3,2,1,0:T(8,128)(2,1)}, u32[]{:S(2)}, u32[]{:S(2)}) %collective-permute-start.13) | collective-permute-done | bytes 196640 | tf_op jit(solution)/shard_map/ppermute | solution.py:265
  86.3 0.0 copy-done.3
  86.3 0.0 copy-done.4
  86.3 0.0 copy-done.5
  86.3 0.0 copy-done.6
  86.3 3.4 %select_pages.3 = bf16[32,2,16,384]{3,2,1,0:T(8,128)(2,1)} custom-call(s32[8,32]{1,0:T(8,128)} %holder_ref.5, bf16[8,2,16,384]{3,2,1,0:T(8,128)(2,1)} %get-tuple-element.23.rest_0_, bf16[8,2,16,384]{3,2,1,0:T(8,128)(2,1)} %copy-done.3, bf16[8,2,16,384]{3,2,1,0:T(8,128)(2,1)} %copy-done.4, bf16[8,2,16,384]{3,2,1,0:T(8,128)(2,1)} %copy-done.5, ...), custom_call_target="tpu_custom_call" | custom-call | bytes 6291456 | tf_op jit(solution)/shard_map/select_pages/pallas_call | solution.py:138
  89.7 4.4 %all-to-all-done.1.pulled_ref = bf16[32,2,16,640]{3,2,1,0:T(8,128)(2,1)} async-done(((bf16[32,2,16,640]{3,2,1,0:T(8,128)(2,1)}), bf16[32,2,16,640]{3,2,1,0:T(8,128)(2,1)}, u32[]{:S(2)}, u32[]{:S(2)}) %all-to-all-start.1) | async-done | bytes 1310752 | tf_op jit(solution)/shard_map/all_to_all | solution.py:269
  94.2 6.8 %all-to-all-start = ((bf16[32,2,16,384]{3,2,1,0:T(8,128)(2,1)}), bf16[32,2,16,384]{3,2,1,0:T(8,128)(2,1)}, u32[]{:S(2)}, u32[]{:S(2)}) async-start(bf16[32,2,16,384]{3,2,1,0:T(8,128)(2,1)} %select_pages.3), calls=%async_computation | async-start | bytes 1572864 | tf_op jit(solution)/shard_map/all_to_all | solution.py:269
  101.0 11.4 %attend.2.rest_0_ = bf16[384,5120]{1,0:T(8,128)(2,1)} custom-call(bf16[384,5120]{1,0:T(8,128)(2,1)} %bitcast.5, bf16[32,2,16,640]{3,2,1,0:T(8,128)(2,1)} %all-to-all-done.1.pulled_ref, bf16[2,384,1024]{2,1,0:T(8,128)(2,1)} %bitcast.7, s32[8,32]{1,0:T(8,128)} %count_ref.3), custom_call_target="tpu_custom_call" | custom-call | flops 3774873600 | bytes 7864320 | tf_op jit(solution)/shard_map/attend/pallas_call | solution.py:250
  112.4 13.5 %all-to-all-done.pulled_ref = bf16[32,2,16,384]{3,2,1,0:T(8,128)(2,1)} async-done(((bf16[32,2,16,384]{3,2,1,0:T(8,128)(2,1)}), bf16[32,2,16,384]{3,2,1,0:T(8,128)(2,1)}, u32[]{:S(2)}, u32[]{:S(2)}) %all-to-all-start) | async-done | bytes 786464 | tf_op jit(solution)/shard_map/all_to_all | solution.py:269
  125.9 7.6 %attend.3 = bf16[384,5120]{1,0:T(8,128)(2,1)} custom-call(bf16[384,5120]{1,0:T(8,128)(2,1)} %bitcast.6, bf16[32,2,16,384]{3,2,1,0:T(8,128)(2,1)} %all-to-all-done.pulled_ref, bf16[2,384,1024]{2,1,0:T(8,128)(2,1)} %bitcast.8, s32[8,32]{1,0:T(8,128)} %count_ref.3, bf16[384,5120]{1,0:T(8,128)(2,1)} %attend.2.rest_0_), custom_call_target="tpu_custom_call", output_to_operand_aliasing={{}: (4, {})} | custom-call | flops 2264924160 | bytes 4718592 | tf_op jit(solution)/shard_map/attend/pallas_call | solution.py:250
  (5 shorter events, 0.0 us)
Async XLA Ops:
  0.0 0.9 copy-start
  6.7 10.9 %collective-permute-start = (bf16[8,2,16,640]{3,2,1,0:T(8,128)(2,1)}, bf16[8,2,16,640]{3,2,1,0:T(8,128)(2,1)S(1)}, u32[]{:S(2)}, u32[]{:S(2)}) collective-permute-start(bf16[8,2,16,640]{3,2,1,0:T(8,128)(2,1)} %get-tuple-element.25), channel_id=1, source_target_pairs={{0,64},{32,96},{64,128},{96,160},{128,192},{160,224},{192,0},{224,... | collective-permute-start | bytes 983048 | tf_op jit(solution)/shard_map/ppermute | solution.py:265
  8.3 12.4 %collective-permute-start.1 = (bf16[8,2,16,640]{3,2,1,0:T(8,128)(2,1)}, bf16[8,2,16,640]{3,2,1,0:T(8,128)(2,1)S(1)}, u32[]{:S(2)}, u32[]{:S(2)}) collective-permute-start(bf16[8,2,16,640]{3,2,1,0:T(8,128)(2,1)} %get-tuple-element.26), channel_id=1, source_target_pairs={{0,192},{32,224},{64,0},{96,32},{128,64},{160,96},{192,128},{224,1... | collective-permute-start | bytes 983048 | tf_op jit(solution)/shard_map/ppermute | solution.py:265
  10.0 11.0 %collective-permute-start.2 = (bf16[8,2,16,640]{3,2,1,0:T(8,128)(2,1)}, bf16[8,2,16,640]{3,2,1,0:T(8,128)(2,1)}, u32[]{:S(2)}, u32[]{:S(2)}) collective-permute-start(bf16[8,2,16,640]{3,2,1,0:T(8,128)(2,1)} %get-tuple-element.27), channel_id=1, source_target_pairs={{0,32},{32,0},{64,96},{96,64},{128,160},{160,128},{192,224},{224,1... | collective-permute-start | bytes 983048 | tf_op jit(solution)/shard_map/ppermute | solution.py:265
  11.4 18.2 %collective-permute-start.3 = (bf16[8,2,16,640]{3,2,1,0:T(8,128)(2,1)}, bf16[8,2,16,640]{3,2,1,0:T(8,128)(2,1)}, u32[]{:S(2)}, u32[]{:S(2)}) collective-permute-start(bf16[8,2,16,640]{3,2,1,0:T(8,128)(2,1)} %get-tuple-element.28), channel_id=1, source_target_pairs={{0,160},{32,128},{64,224},{96,192},{128,32},{160,0},{192,96},{224,... | collective-permute-start | bytes 983048 | tf_op jit(solution)/shard_map/ppermute | solution.py:265
  13.2 23.0 %collective-permute-start.4 = (bf16[8,2,16,640]{3,2,1,0:T(8,128)(2,1)}, bf16[8,2,16,640]{3,2,1,0:T(8,128)(2,1)}, u32[]{:S(2)}, u32[]{:S(2)}) collective-permute-start(bf16[8,2,16,640]{3,2,1,0:T(8,128)(2,1)} %get-tuple-element.29), channel_id=1, source_target_pairs={{0,96},{32,64},{64,160},{96,128},{128,224},{160,192},{192,32},{224... | collective-permute-start | bytes 983048 | tf_op jit(solution)/shard_map/ppermute | solution.py:265
  17.6 25.4 %copy-start.1 = (bf16[8,2,16,640]{3,2,1,0:T(8,128)(2,1)}, bf16[8,2,16,640]{3,2,1,0:T(8,128)(2,1)S(1)}, u32[]{:S(2)}) copy-start(bf16[8,2,16,640]{3,2,1,0:T(8,128)(2,1)S(1)} %collective-permute-done.rest_1_) | copy-start | bytes 983044
  17.6 25.3 %collective-permute-start.5 = (bf16[8,2,16,640]{3,2,1,0:T(8,128)(2,1)}, bf16[8,2,16,640]{3,2,1,0:T(8,128)(2,1)}, u32[]{:S(2)}, u32[]{:S(2)}) collective-permute-start(bf16[8,2,16,640]{3,2,1,0:T(8,128)(2,1)} %get-tuple-element.30), channel_id=1, source_target_pairs={{0,224},{32,192},{64,32},{96,0},{128,96},{160,64},{192,160},{224,1... | collective-permute-start | bytes 983048 | tf_op jit(solution)/shard_map/ppermute | solution.py:265
  20.7 22.3 %copy-start.2 = (bf16[8,2,16,640]{3,2,1,0:T(8,128)(2,1)}, bf16[8,2,16,640]{3,2,1,0:T(8,128)(2,1)S(1)}, u32[]{:S(2)}) copy-start(bf16[8,2,16,640]{3,2,1,0:T(8,128)(2,1)S(1)} %collective-permute-done.1.rest_2_) | copy-start | bytes 983044
  20.7 22.3 %collective-permute-start.6 = (bf16[8,2,16,640]{3,2,1,0:T(8,128)(2,1)}, bf16[8,2,16,640]{3,2,1,0:T(8,128)(2,1)}, u32[]{:S(2)}, u32[]{:S(2)}) collective-permute-start(bf16[8,2,16,640]{3,2,1,0:T(8,128)(2,1)} %get-tuple-element.31), channel_id=1, source_target_pairs={{0,128},{32,160},{64,192},{96,224},{128,0},{160,32},{192,64},{224,... | collective-permute-start | bytes 983048 | tf_op jit(solution)/shard_map/ppermute | solution.py:265
  20.9 25.8 %collective-permute-start.7 = (bf16[8,2,16,384]{3,2,1,0:T(8,128)(2,1)}, bf16[8,2,16,384]{3,2,1,0:T(8,128)(2,1)S(1)}, u32[]{:S(2)}, u32[]{:S(2)}) collective-permute-start(bf16[8,2,16,384]{3,2,1,0:T(8,128)(2,1)} %get-tuple-element.32), channel_id=1, source_target_pairs={{0,32},{32,0},{64,96},{96,64},{128,160},{160,128},{192,224},{224,1... | collective-permute-start | bytes 589832 | tf_op jit(solution)/shard_map/ppermute | solution.py:265
  46.8 39.5 %copy-start.3 = (bf16[8,2,16,384]{3,2,1,0:T(8,128)(2,1)}, bf16[8,2,16,384]{3,2,1,0:T(8,128)(2,1)S(1)}, u32[]{:S(2)}) copy-start(bf16[8,2,16,384]{3,2,1,0:T(8,128)(2,1)S(1)} %collective-permute-done.7.rest_1_) | copy-start | bytes 589828
  46.8 47.4 %all-to-all-start.1 = ((bf16[32,2,16,640]{3,2,1,0:T(8,128)(2,1)}), bf16[32,2,16,640]{3,2,1,0:T(8,128)(2,1)}, u32[]{:S(2)}, u32[]{:S(2)}) async-start(bf16[32,2,16,640]{3,2,1,0:T(8,128)(2,1)} %select_pages.2), calls=%async_computation.1 | async-start | bytes 2621440 | tf_op jit(solution)/shard_map/all_to_all | solution.py:269
  58.0 13.8 %collective-permute-start.8 = (bf16[8,2,16,384]{3,2,1,0:T(8,128)(2,1)}, bf16[8,2,16,384]{3,2,1,0:T(8,128)(2,1)S(1)}, u32[]{:S(2)}, u32[]{:S(2)}) collective-permute-start(bf16[8,2,16,384]{3,2,1,0:T(8,128)(2,1)} %get-tuple-element.34), channel_id=1, source_target_pairs={{0,64},{32,96},{64,128},{96,160},{128,192},{160,224},{192,0},{224,... | collective-permute-start | bytes 589832 | tf_op jit(solution)/shard_map/ppermute | solution.py:265
  58.9 13.9 %collective-permute-start.9 = (bf16[8,2,16,384]{3,2,1,0:T(8,128)(2,1)}, bf16[8,2,16,384]{3,2,1,0:T(8,128)(2,1)S(1)}, u32[]{:S(2)}, u32[]{:S(2)}) collective-permute-start(bf16[8,2,16,384]{3,2,1,0:T(8,128)(2,1)} %get-tuple-element.35), channel_id=1, source_target_pairs={{0,96},{32,64},{64,160},{96,128},{128,224},{160,192},{192,32},{224... | collective-permute-start | bytes 589832 | tf_op jit(solution)/shard_map/ppermute | solution.py:265
  59.9 19.0 %collective-permute-start.10 = (bf16[8,2,16,384]{3,2,1,0:T(8,128)(2,1)}, bf16[8,2,16,384]{3,2,1,0:T(8,128)(2,1)S(1)}, u32[]{:S(2)}, u32[]{:S(2)}) collective-permute-start(bf16[8,2,16,384]{3,2,1,0:T(8,128)(2,1)} %get-tuple-element.36), channel_id=1, source_target_pairs={{0,128},{32,160},{64,192},{96,224},{128,0},{160,32},{192,64},{224,... | collective-permute-start | bytes 589832 | tf_op jit(solution)/shard_map/ppermute | solution.py:265
  63.0 17.5 %collective-permute-start.11 = (bf16[8,2,16,384]{3,2,1,0:T(8,128)(2,1)}, bf16[8,2,16,384]{3,2,1,0:T(8,128)(2,1)}, u32[]{:S(2)}, u32[]{:S(2)}) collective-permute-start(bf16[8,2,16,384]{3,2,1,0:T(8,128)(2,1)} %get-tuple-element.37), channel_id=1, source_target_pairs={{0,160},{32,128},{64,224},{96,192},{128,32},{160,0},{192,96},{224,... | collective-permute-start | bytes 589832 | tf_op jit(solution)/shard_map/ppermute | solution.py:265
  64.3 16.1 %collective-permute-start.12 = (bf16[8,2,16,384]{3,2,1,0:T(8,128)(2,1)}, bf16[8,2,16,384]{3,2,1,0:T(8,128)(2,1)}, u32[]{:S(2)}, u32[]{:S(2)}) collective-permute-start(bf16[8,2,16,384]{3,2,1,0:T(8,128)(2,1)} %get-tuple-element.38), channel_id=1, source_target_pairs={{0,192},{32,224},{64,0},{96,32},{128,64},{160,96},{192,128},{224,1... | collective-permute-start | bytes 589832 | tf_op jit(solution)/shard_map/ppermute | solution.py:265
  71.9 14.4 %copy-start.4 = (bf16[8,2,16,384]{3,2,1,0:T(8,128)(2,1)}, bf16[8,2,16,384]{3,2,1,0:T(8,128)(2,1)S(1)}, u32[]{:S(2)}) copy-start(bf16[8,2,16,384]{3,2,1,0:T(8,128)(2,1)S(1)} %collective-permute-done.8.rest_2_) | copy-start | bytes 589828
  71.9 14.4 %collective-permute-start.13 = (bf16[8,2,16,384]{3,2,1,0:T(8,128)(2,1)}, bf16[8,2,16,384]{3,2,1,0:T(8,128)(2,1)}, u32[]{:S(2)}, u32[]{:S(2)}) collective-permute-start(bf16[8,2,16,384]{3,2,1,0:T(8,128)(2,1)} %get-tuple-element.39), channel_id=1, source_target_pairs={{0,224},{32,192},{64,32},{96,0},{128,96},{160,64},{192,160},{224,1... | collective-permute-start | bytes 589832 | tf_op jit(solution)/shard_map/ppermute | solution.py:265
  72.9 13.4 %copy-start.5 = (bf16[8,2,16,384]{3,2,1,0:T(8,128)(2,1)}, bf16[8,2,16,384]{3,2,1,0:T(8,128)(2,1)S(1)}, u32[]{:S(2)}) copy-start(bf16[8,2,16,384]{3,2,1,0:T(8,128)(2,1)S(1)} %collective-permute-done.9.rest_3_) | copy-start | bytes 589828
  78.8 7.5 %copy-start.6 = (bf16[8,2,16,384]{3,2,1,0:T(8,128)(2,1)}, bf16[8,2,16,384]{3,2,1,0:T(8,128)(2,1)S(1)}, u32[]{:S(2)}) copy-start(bf16[8,2,16,384]{3,2,1,0:T(8,128)(2,1)S(1)} %collective-permute-done.10.rest_4_) | copy-start | bytes 589828
  94.2 31.7 %all-to-all-start = ((bf16[32,2,16,384]{3,2,1,0:T(8,128)(2,1)}), bf16[32,2,16,384]{3,2,1,0:T(8,128)(2,1)}, u32[]{:S(2)}, u32[]{:S(2)}) async-start(bf16[32,2,16,384]{3,2,1,0:T(8,128)(2,1)} %select_pages.3), calls=%async_computation | async-start | bytes 1572864 | tf_op jit(solution)/shard_map/all_to_all | solution.py:269
